TPU v7x, 32 devices: a whole 2x2x4 slice. The times are simulated.
32 devices in a mesh: expert: 16 (over z, y, core), dp: 2 (over x).
Axes of the slice: x: 2, y: 2, z: 4, core: 2. Of those that a mesh axis runs over, the one named last changes fastest.
Arguments:
- tokens: bfloat16 [4096, 2048], P(('dp', 'expert')), parts along dimension 0, may hold values from -6 to 6
- expert_ids: int32 [4096, 8], P(('dp', 'expert')), parts along dimension 0, may hold values from 0 to 15, all different within a row; in each aligned block of 128 rows (0 to 127, 128 to 255, ...) at most 72 rows name the same one
- route_weight: float32 [4096, 8], P(('dp', 'expert')), parts along dimension 0, may hold values from 0.05 to 1
- w_gate: bfloat16 [16, 2, 2048, 384], P('expert'), may hold values from -0.125 to 0.125
- w_up: bfloat16 [16, 2, 2048, 384], P('expert'), may hold values from -0.125 to 0.125
- w_down: bfloat16 [16, 2, 384, 2048], P('expert'), may hold values from -0.21875 to 0.21875
Outputs:
- mixed: bfloat16 [4096, 2048], P(('dp', 'expert')), parts along dimension 0
There are 2 independent parts, one for each index of `dp`. A program takes and returns all parts, laid end to end along the dimension named above; an argument that names none is the same for every part. Nothing has to cross between parts.
Inputs may be any that keep to these rules, and one draw needn't show every extreme that they name: `expert_ids`: each row names 8 different experts. In the rows of one device (aligned blocks of 128 rows) no expert is named by more than 72 rows, a bound that some block reaches.
All inputs are finite; a program needn't handle non-finite values.
Results may differ from a plain program's by a relative error of at most 0.0071.
Values may be sent and summed in bfloat16 or wider, within the bound.
A program may use at most 128 MiB of HBM per device.

v0:
```python
import jax
import jax.numpy as jnp
from jax import lax
from jax.sharding import PartitionSpec as P


def partner(value, axis, bit):
    mask = 2**bit
    pairs = [(source, source ^ mask) for source in range(lax.axis_size(axis))]
    return lax.ppermute(value, axis, pairs)


def whole_expert(rows, gates, gate_both, up_both, down_both):
    gate_h = jnp.einsum("scd,hdf->shcf", rows, gate_both, preferred_element_type=jnp.float32)
    up_h = jnp.einsum("scd,hdf->shcf", rows, up_both, preferred_element_type=jnp.float32)
    hidden = (jax.nn.silu(gate_h) * up_h).astype(jnp.bfloat16)
    partial_value = jnp.einsum(
        "shcf,hfd->shcd", hidden, down_both, preferred_element_type=jnp.float32
    )
    partial_value = (partial_value * gates.astype(jnp.float32)[:, None, :, None]).astype(
        jnp.bfloat16
    )
    return (
        partial_value[:, 0].astype(jnp.float32) + partial_value[:, 1].astype(jnp.float32)
    ).astype(jnp.bfloat16)


def on_device(tokens, expert_ids, route_weight, w_gate, w_up, w_down):
    devices_n = lax.axis_size("expert")
    parity = lax.axis_index("expert") % 2
    tok_rows = tokens.shape[0]
    top_n = expert_ids.shape[1]
    width = tokens.shape[1]
    slots = tok_rows * top_n * 9 // (8 * devices_n)
    weight_g = w_gate[0]
    weight_u = w_up[0]
    weight_d = w_down[0]
    gates = (route_weight / jnp.sum(route_weight, axis=1, keepdims=True)).astype(jnp.bfloat16)
    flat_ids = expert_ids.reshape(-1)
    onehot = (flat_ids[:, None] == jnp.arange(devices_n, dtype=jnp.int32)[None, :]).astype(
        jnp.int32
    )
    before = jnp.cumsum(onehot, axis=0) - onehot
    slot = jnp.sum(before * onehot, axis=1)
    position = flat_ids * slots + slot
    token_index = jnp.arange(tok_rows * top_n, dtype=jnp.int32) // top_n
    table_tok = jnp.zeros((devices_n * slots,), jnp.int32).at[position].set(token_index)
    table_live = (
        jnp.zeros((devices_n * slots,), jnp.bfloat16)
        .at[position]
        .set(jnp.ones((tok_rows * top_n,), jnp.bfloat16))
    )
    table_gate = jnp.zeros((devices_n * slots,), jnp.bfloat16).at[position].set(gates.reshape(-1))
    send_rows = (tokens[table_tok] * table_live[:, None]).reshape(devices_n, slots, width)
    send_gate = table_gate.reshape(devices_n, slots)
    other_g, other_u, other_d = partner((weight_g, weight_u, weight_d), "expert", 0)
    own_rows, own_gate = (
        lax.all_to_all(send_rows, "expert", split_axis=0, concat_axis=0, tiled=True),
        lax.all_to_all(send_gate, "expert", split_axis=0, concat_axis=0, tiled=True),
    )
    even = parity == 0
    mine_g = lax.dynamic_index_in_dim(weight_g, parity, 0, keepdims=False)
    mine_u = lax.dynamic_index_in_dim(weight_u, parity, 0, keepdims=False)
    mine_d = lax.dynamic_index_in_dim(weight_d, parity, 0, keepdims=False)
    theirs_g = lax.dynamic_index_in_dim(other_g, parity, 0, keepdims=False)
    theirs_u = lax.dynamic_index_in_dim(other_u, parity, 0, keepdims=False)
    theirs_d = lax.dynamic_index_in_dim(other_d, parity, 0, keepdims=False)
    gate_both = jnp.where(even, jnp.stack([mine_g, theirs_g]), jnp.stack([theirs_g, mine_g]))
    up_both = jnp.where(even, jnp.stack([mine_u, theirs_u]), jnp.stack([theirs_u, mine_u]))
    down_both = jnp.where(even, jnp.stack([mine_d, theirs_d]), jnp.stack([theirs_d, mine_d]))
    outputs = whole_expert(own_rows, own_gate, gate_both, up_both, down_both)
    combined = lax.all_to_all(outputs, "expert", split_axis=0, concat_axis=0, tiled=True).reshape(
        devices_n * slots, width
    )
    picked = combined[position].reshape(tok_rows, top_n, width)
    return jnp.sum(picked.astype(jnp.float32), axis=1).astype(jnp.bfloat16)


def solution(mesh):
    return jax.shard_map(
        on_device,
        mesh=mesh,
        in_specs=(
            P(("dp", "expert"), None),
            P(("dp", "expert"), None),
            P(("dp", "expert"), None),
            P("expert", None, None, None),
            P("expert", None, None, None),
            P("expert", None, None, None),
        ),
        out_specs=P(("dp", "expert"), None),
        check_vma=False,
    )
```

profile of v0, /device:TPU:13, one launch (start us, length us, event | category | flops | bytes accessed | tf_op | source)
XLA Modules:
  0.0 325.5 jit_solution(13702573022947065445)
XLA Ops:
  0.0 0.7 broadcast_multiply_fusion.1
  0.8 0.8 copy.22
  1.7 0.7 reduce_sum.34
  2.4 0.7 divide_convert_fusion
  3.6 4.5 %reduce-window.6 = s32[16,8,128]{2,1,0:T(8,128)S(1)} reduce-window(s32[16,8,128]{2,1,0:T(8,128)S(1)} %fusion.45, s32[]{:T(128)} %constant.64.clone.1), window={size=1x1x128 pad=0_0x0_0x127_0}, to_apply=%region_0.1 | reduce-window | flops 2080768 | bytes 131076 | tf_op jit(solution)/shard_map/reduce-window
  8.2 0.1 copy.24
  8.6 7.6 %scatter_custom_fusion.2 = bf16[1152]{0:T(1024)(128)(2,1)S(1)} fusion(s32[1024]{0:T(1024)S(1)} %bitcast.97, bf16[1024]{0:T(1024)(128)(2,1)S(1)} %reshape.123, bf16[]{:T(256)} %constant.73.clone.1), kind=kCustom, calls=%fused_computation.71 | custom fusion | bytes 2306 | tf_op jit(solution)/shard_map/scatter | solution.py:53
  16.2 0.7 all_to_all.16
  16.9 6.6 %all-to-all-start.1 = ((bf16[16,1,72]{2,1,0:T(2,128)(2,1)}), bf16[16,1,72]{2,1,0:T(2,128)(2,1)S(1)}, u32[]{:S(2)}, u32[]{:S(2)}) async-start(bf16[16,1,72]{2,1,0:T(2,128)(2,1)} %all_to_all.16), calls=%async_computation.1 | async-start | bytes 16384 | tf_op jit(solution)/shard_map/all_to_all | solution.py:59
  23.4 7.6 %scatter_custom_fusion.1 = bf16[1152]{0:T(1024)(128)(2,1)S(1)} fusion(s32[1024]{0:T(1024)S(1)} %bitcast.98, bf16[1024]{0:T(1024)(128)(2,1)S(1)} %broadcast.72, bf16[]{:T(256)} %constant.73.clone.1), kind=kCustom, calls=%fused_computation.73 | custom fusion | bytes 2306 | tf_op jit(solution)/shard_map/scatter | solution.py:51
  31.1 4.3 %scatter_custom_fusion = s32[1152]{0:T(1024)S(1)} fusion(s32[1024]{0:T(1024)S(1)} %bitcast.99, s32[1024]{0:T(1024)S(1)} %add_select_fusion, s32[]{:T(128)} %constant.64.clone.1), kind=kCustom, calls=%fused_computation.67 | custom fusion | bytes 4612 | tf_op jit(solution)/shard_map/scatter | solution.py:47
  35.5 6.0 %gather_fusion = bf16[1152,2048]{1,0:T(8,128)(2,1)} fusion(bf16[128,2048]{1,0:T(8,128)(2,1)S(1)} %copy-done, s32[2048]{0:T(1024)S(1)} %pad_clamp_fusion), kind=kCustom, calls=%fused_computation | custom fusion | bytes 9441792 | tf_op jit(solution)/shard_map/gather | solution.py:54
  41.5 4.8 %broadcast_multiply_fusion = bf16[16,72,2048]{2,1,0:T(8,128)(2,1)} fusion(bf16[16,72,2048]{2,1,0:T(8,128)(2,1)} %bitcast.90, bf16[16,72]{1,0:T(8,128)(2,1)S(1)} %mul.50), kind=kLoop, calls=%fused_computation.45 | loop fusion | flops 2359296 | bytes 9439488 | tf_op jit(solution)/shard_map/mul | solution.py:54
  46.3 6.0 %all-to-all-start = ((bf16[16,72,2048]{2,1,0:T(8,128)(2,1)}), bf16[16,72,2048]{2,1,0:T(8,128)(2,1)}, u32[]{:S(2)}, u32[]{:S(2)}) async-start(bf16[16,72,2048]{2,1,0:T(8,128)(2,1)} %broadcast_multiply_fusion), calls=%async_computation | async-start | bytes 9437184 | tf_op jit(solution)/shard_map/all_to_all | solution.py:58
  52.4 0.4 collective-permute-start
  52.8 0.1 collective-permute-start.2
  52.9 0.4 collective-permute-start.1
  53.3 1.5 dynamic-slice_bitcast_fusion.2
  54.8 3.9 %dynamic-slice_bitcast_fusion = (bf16[1,2048,384]{2,1,0:T(8,128)(2,1)}, bf16[1,2048,384]{2,1,0:T(8,128)(2,1)}) fusion(bf16[1,2,2048,384]{3,2,1,0:T(8,128)(2,1)} %param.10, s32[]{:T(128)S(6)} %select_n.60, bf16[1,2,2048,384]{3,2,1,0:T(8,128)(2,1)} %param.9), kind=kLoop, calls=%fused_computation.46 | loop fusion | bytes 6291460 | tf_op jit(solution)/shard_map/jit(dynamic_index_in_dim)/dynamic_slice | solution.py:63
  58.7 2.8 constant_dynamic-slice_fusion.2
  61.5 1.6 collective-permute-done.2
  63.1 2.7 constant_dynamic-slice_fusion
  65.9 1.8 collective-permute-done.1
  67.6 2.7 constant_dynamic-slice_fusion.1
  70.3 85.7 %all-to-all-done = bf16[16,72,2048]{2,1,0:T(8,128)(2,1)} async-done(((bf16[16,72,2048]{2,1,0:T(8,128)(2,1)}), bf16[16,72,2048]{2,1,0:T(8,128)(2,1)}, u32[]{:S(2)}, u32[]{:S(2)}) %all-to-all-start) | async-done | bytes 4718624 | tf_op jit(solution)/shard_map/all_to_all | solution.py:58
  156.1 9.8 %fusion.4 = f32[2,384,16,72]{1,3,2,0:T(8,128)} fusion(bf16[16,72,2048]{2,1,0:T(8,128)(2,1)} %all-to-all-done, bf16[1,2048,384]{2,1,0:T(8,128)(2,1)} %constant_dynamic-slice_fusion.1, bf16[1,2048,384]{2,1,0:T(8,128)(2,1)} %get-tuple-element.6, pred[]{:T(512)S(6)} %eq.30), kind=kOutput, calls=%fused_computation.11 | convolution fusion | flops 3638034432 | bytes 11403265 | tf_op jit(solution)/shard_map/scd,hdf->shcf/dot_general | solution.py:14
  165.9 24.6 %fusion = bf16[16,2,72,2048]{3,2,0,1:T(8,128)(2,1)} fusion(f32[16,72]{1,0:T(8,128)S(1)} %bitcast.101, bf16[1,384,2048]{2,1,0:T(8,128)(2,1)} %constant_dynamic-slice_fusion.2, bf16[1,384,2048]{2,1,0:T(8,128)(2,1)S(1)} %dynamic-slice_bitcast_fusion.2, pred[]{:T(512)S(6)} %eq.30, f32[2,384,16,72]{1,3,2,0:T(8,128)} %fusion.4, ...), kind=kOutput, calls=%fused_computation.6 | convolution fusion | flops 7290814464 | bytes 23990784 | tf_op jit(solution)/shard_map/shcf,hfd->shcd/dot_general | solution.py:17
  190.5 8.7 %fusion.1 = bf16[16,72,2048]{2,1,0:T(8,128)(2,1)} fusion(bf16[16,2,72,2048]{3,2,0,1:T(8,128)(2,1)} %fusion), kind=kLoop, calls=%fused_computation.8 | loop fusion | flops 9437184 | bytes 14155776 | tf_op jit(solution)/shard_map/convert_element_type | solution.py:25
  199.2 4.9 %all-to-all-start.2 = ((bf16[16,72,2048]{2,1,0:T(8,128)(2,1)}), bf16[16,72,2048]{2,1,0:T(8,128)(2,1)}, u32[]{:S(2)}, u32[]{:S(2)}) async-start(bf16[16,72,2048]{2,1,0:T(8,128)(2,1)} %fusion.1), calls=%async_computation.2 | async-start | bytes 9437184 | tf_op jit(solution)/shard_map/all_to_all | solution.py:72
  204.1 103.7 %all-to-all-done.2 = bf16[16,72,2048]{2,1,0:T(8,128)(2,1)} async-done(((bf16[16,72,2048]{2,1,0:T(8,128)(2,1)}), bf16[16,72,2048]{2,1,0:T(8,128)(2,1)}, u32[]{:S(2)}, u32[]{:S(2)}) %all-to-all-start.2) | async-done | bytes 4718624 | tf_op jit(solution)/shard_map/all_to_all | solution.py:72
  307.8 11.9 %gather_fusion.1 = bf16[1024,2048]{1,0:T(8,128)(2,1)} fusion(bf16[1152,2048]{1,0:T(8,128)(2,1)} %bitcast.23, s32[1024]{0:T(1024)S(1)} %broadcast_clamp_fusion), kind=kCustom, calls=%fused_computation.1 | custom fusion | bytes 8392704 | tf_op jit(solution)/shard_map/gather | solution.py:75
  319.7 5.9 %bitcast_reduce_fusion = bf16[128,2048]{1,0:T(8,128)(2,1)} fusion(bf16[1024,2048]{1,0:T(8,128)(2,1)} %gather_fusion.1), kind=kLoop, calls=%fused_computation.13 | loop fusion | flops 1835008 | bytes 4718592 | tf_op jit(solution)/shard_map/reduce_sum | solution.py:76
  (27 shorter events, 1.1 us)
Async XLA Ops:
  0.0 35.5 %copy-start = (bf16[128,2048]{1,0:T(8,128)(2,1)S(1)}, bf16[128,2048]{1,0:T(8,128)(2,1)}, u32[]{:S(2)}) copy-start(bf16[128,2048]{1,0:T(8,128)(2,1)} %param.6) | copy-start | bytes 1572868
  16.9 29.5 %all-to-all-start.1 = ((bf16[16,1,72]{2,1,0:T(2,128)(2,1)}), bf16[16,1,72]{2,1,0:T(2,128)(2,1)S(1)}, u32[]{:S(2)}, u32[]{:S(2)}) async-start(bf16[16,1,72]{2,1,0:T(2,128)(2,1)} %all_to_all.16), calls=%async_computation.1 | async-start | bytes 16384 | tf_op jit(solution)/shard_map/all_to_all | solution.py:59
  46.3 109.7 %all-to-all-start = ((bf16[16,72,2048]{2,1,0:T(8,128)(2,1)}), bf16[16,72,2048]{2,1,0:T(8,128)(2,1)}, u32[]{:S(2)}, u32[]{:S(2)}) async-start(bf16[16,72,2048]{2,1,0:T(8,128)(2,1)} %broadcast_multiply_fusion), calls=%async_computation | async-start | bytes 9437184 | tf_op jit(solution)/shard_map/all_to_all | solution.py:58
  52.4 6.4 %collective-permute-start = (bf16[2,384,2048]{2,1,0:T(8,128)(2,1)}, bf16[2,384,2048]{2,1,0:T(8,128)(2,1)}, u32[]{:S(2)}, u32[]{:S(2)}) collective-permute-start(bf16[2,384,2048]{2,1,0:T(8,128)(2,1)} %bitcast.91), channel_id=1, source_target_pairs={{0,2},{2,0},{4,6},{6,4},{8,10},{10,8},{12,14},{14,12},{16,18},{18,... | collective-permute-start | bytes 9437192 | tf_op jit(solution)/shard_map/ppermute | solution.py:10
  52.8 10.3 %collective-permute-start.2 = (bf16[2,2048,384]{2,1,0:T(8,128)(2,1)}, bf16[2,2048,384]{2,1,0:T(8,128)(2,1)}, u32[]{:S(2)}, u32[]{:S(2)}) collective-permute-start(bf16[2,2048,384]{2,1,0:T(8,128)(2,1)} %bitcast.92), channel_id=1, source_target_pairs={{0,2},{2,0},{4,6},{6,4},{8,10},{10,8},{12,14},{14,12},{16,18},{18,... | collective-permute-start | bytes 9437192 | tf_op jit(solution)/shard_map/ppermute | solution.py:10
  52.9 14.7 %collective-permute-start.1 = (bf16[2,2048,384]{2,1,0:T(8,128)(2,1)}, bf16[2,2048,384]{2,1,0:T(8,128)(2,1)}, u32[]{:S(2)}, u32[]{:S(2)}) collective-permute-start(bf16[2,2048,384]{2,1,0:T(8,128)(2,1)} %bitcast.93), channel_id=1, source_target_pairs={{0,2},{2,0},{4,6},{6,4},{8,10},{10,8},{12,14},{14,12},{16,18},{18,... | collective-permute-start | bytes 9437192 | tf_op jit(solution)/shard_map/ppermute | solution.py:10
  199.2 108.6 %all-to-all-start.2 = ((bf16[16,72,2048]{2,1,0:T(8,128)(2,1)}), bf16[16,72,2048]{2,1,0:T(8,128)(2,1)}, u32[]{:S(2)}, u32[]{:S(2)}) async-start(bf16[16,72,2048]{2,1,0:T(8,128)(2,1)} %fusion.1), calls=%async_computation.2 | async-start | bytes 9437184 | tf_op jit(solution)/shard_map/all_to_all | solution.py:72
  307.8 17.7 %copy-start.1 = (bf16[128,2048]{1,0:T(8,128)(2,1)S(1)}, bf16[128,2048]{1,0:T(8,128)(2,1)}, u32[]{:S(2)}) copy-start(bf16[128,2048]{1,0:T(8,128)(2,1)} %param.6) | copy-start | bytes 1572868
where the time goes:
time: 326 us
  waiting for transfers between devices  193 us (59%)
  local copies, waits for them, and re-layouts  53.5 us (16%)
  matrix products  34.5 us (11%)
  other arithmetic  26.2 us (8%)
  starting transfers between devices  18.4 us (6%)
    all_to_all x1, waiting for transfers between devices, on_device(): lax.all_to_all(outputs, 'expert', split_axis=0, concat_axis=0, tiled=True)  104 us
    all_to_all x1, waiting for transfers between devices, on_device(): lax.all_to_all(send_rows, 'expert', split_axis=0, concat_axis=0, tiled=True)  85.7 us
    dot_general x1, matrix products, whole_expert(): jnp.einsum('shcf,hfd->shcd', hidden, down_both, preferred_element_type=jn...  24.6 us
    gather x1, local copies, waits for them, and re-layouts, on_device(): picked = combined[position].reshape(tok_rows, top_n, width)  11.9 us
    dot_general x1, matrix products, whole_expert(): jnp.einsum('scd,hdf->shcf', rows, gate_both, preferred_element_type=jnp.f...  9.83 us
    convert_element_type x1, other arithmetic, whole_expert(): return (partial_value[:, 0].astype(jnp.float32) + partial_value[:, 1].ast...  8.65 us
    scatter x1, local copies, waits for them, and re-layouts, on_device(): jnp.zeros((devices_n * slots,), jnp.bfloat16).at[position]  7.59 us
    scatter x1, local copies, waits for them, and re-layouts, on_device(): table_live = jnp.zeros((devices_n * slots,), jnp.bfloat16).at[position].s...  7.59 us
  transfers between devices with their start and end apart: 6, of which 4 were waited for; matrix products, arithmetic and copies ran while one was open for 11% of the time, Pallas kernels for 0%

commit v1 on v0

v1 whole, which is shorter than its diff:
```python
import functools

import jax
import jax.numpy as jnp
from jax import lax
from jax.experimental import pallas as pl
from jax.experimental.pallas import tpu as pltpu
from jax.sharding import PartitionSpec as P


def chip_cycle(chips_n, rows_n):
    if rows_n % 2 or chips_n % rows_n or chips_n // rows_n < 2:
        return list(range(chips_n))
    deep = chips_n // rows_n
    walk = []
    for y in range(rows_n):
        zs = range(1, deep) if y % 2 == 0 else range(deep - 1, 0, -1)
        walk += [z * rows_n + y for z in zs]
    return walk + list(range(rows_n - 1, -1, -1))


def ffn_kernel(x_ref, gate_ref, g0, u0, d0, g1, u1, d1, out_ref):
    i = pl.program_id(0)
    x = x_ref[...]
    weight = jnp.where(i % 2 == 0, gate_ref[:, 0:1], gate_ref[:, 1:2])

    def add(g_ref, u_ref, d_ref, first):
        gate_h = jnp.dot(x, g_ref[0], preferred_element_type=jnp.float32)
        up_h = jnp.dot(x, u_ref[0], preferred_element_type=jnp.float32)
        hidden = gate_h / (1.0 + jnp.exp(-gate_h)) * up_h
        hidden = hidden.astype(jnp.bfloat16)
        part = jnp.dot(hidden, d_ref[0], preferred_element_type=jnp.float32) * weight

        if first:

            @pl.when(i == 0)
            def _():
                out_ref[...] = part

            @pl.when(i > 0)
            def _():
                out_ref[...] += part

        else:
            out_ref[...] += part

    @pl.when(i < 2)
    def _():
        add(g0, u0, d0, True)

    @pl.when(i >= 2)
    def _():
        add(g1, u1, d1, False)


def ffn(x, gates, own, other):
    rows, width = x.shape
    half = own[0].shape[2]

    def early(shape):
        return pl.BlockSpec((1,) + shape, lambda i: (jnp.minimum(i, 1), 0, 0))

    def late(shape):
        return pl.BlockSpec((1,) + shape, lambda i: (jnp.maximum(i - 2, 0), 0, 0))

    flops = 4 * 2 * 3 * rows * width * half
    moved = 4 * 3 * width * half * 2 + rows * width * 6
    return pl.pallas_call(
        ffn_kernel,
        grid=(4,),
        out_shape=jax.ShapeDtypeStruct((rows, width), jnp.float32),
        in_specs=[
            pl.BlockSpec((rows, width), lambda i: (0, 0)),
            pl.BlockSpec((rows, 2), lambda i: (0, 0)),
            early((width, half)),
            early((width, half)),
            early((half, width)),
            late((width, half)),
            late((width, half)),
            late((half, width)),
        ],
        out_specs=pl.BlockSpec((rows, width), lambda i: (0, 0)),
        cost_estimate=pl.CostEstimate(
            flops=flops, bytes_accessed=moved, transcendentals=4 * rows * half
        ),
        compiler_params=pltpu.CompilerParams(vmem_limit_bytes=48 * 2**20),
    )(x, gates, *own, *other)


def on_device(cycle, tokens, expert_ids, route_weight, w_gate, w_up, w_down):
    devices_n = lax.axis_size("expert")
    index = lax.axis_index("expert")
    chips_n = devices_n // 2
    chip, core = index // 2, index % 2
    rows = tokens.shape[0]
    cut = rows // 2
    far = chips_n // 2
    place = [0] * chips_n
    for i, c in enumerate(cycle):
        place[c] = i

    def turn(step):
        pairs = []
        for i, c in enumerate(cycle):
            to = cycle[(i + step) % chips_n]
            pairs += [(2 * c, 2 * to), (2 * c + 1, 2 * to + 1)]
        return pairs

    right, left = turn(1), turn(-1)
    swap = [(i, i ^ 1) for i in range(devices_n)]
    send = lambda value, pairs: lax.ppermute(value, "expert", pairs)

    gates = (route_weight / jnp.sum(route_weight, axis=1, keepdims=True)).astype(jnp.bfloat16)
    chosen = expert_ids[:, :, None] == jnp.arange(devices_n, dtype=jnp.int32)
    dense = jnp.sum(jnp.where(chosen, gates.astype(jnp.float32)[:, :, None], 0.0), axis=1)

    own = (w_gate[0], w_up[0], w_down[0])
    other = tuple(send(w, swap) for w in own)
    all_gates = lax.all_gather(dense.astype(jnp.bfloat16), "expert")
    all_gates = all_gates.reshape(chips_n, 2, rows, devices_n)
    all_gates = lax.dynamic_index_in_dim(all_gates, core, 1, keepdims=False)
    all_gates = lax.dynamic_slice_in_dim(all_gates, 2 * chip, 2, 2).astype(jnp.float32)
    here = jnp.array(place, jnp.int32)[chip]
    walk = jnp.array(cycle, jnp.int32)

    def gates_at(distance):
        return lax.dynamic_index_in_dim(
            all_gates, walk[(here + distance + chips_n) % chips_n], 0, keepdims=False
        )

    from_left, from_right = {0: tokens}, {0: tokens}
    for s in range(1, far):
        from_left[s] = send(from_left[s - 1], right)
        from_right[s] = send(from_right[s - 1], left)
    far_block = jnp.concatenate(
        [send(from_left[far - 1][:cut], right), send(from_right[far - 1][cut:], left)]
    )

    def outputs(blocks, distances):
        x = jnp.concatenate(blocks) if len(blocks) > 1 else blocks[0]
        g = jnp.concatenate([gates_at(d) for d in distances])
        return ffn(x, g, own, other)

    near = outputs([from_left[1], from_right[1], tokens], [-1, 1, 0])
    for_left, for_right = {1: near[:rows]}, {1: near[rows : 2 * rows]}
    mine = near[2 * rows :]
    for s in range(2, far):
        both = outputs([from_left[s], from_right[s]], [-s, s])
        for_left[s], for_right[s] = both[:rows], both[rows:]
    last = outputs([far_block], [far])

    to_right = send(last[:cut].astype(jnp.bfloat16), right)
    to_left = send(last[cut:].astype(jnp.bfloat16), left)
    to_right = jnp.pad(to_right, ((0, cut), (0, 0)))
    to_left = jnp.pad(to_left, ((cut, 0), (0, 0)))
    for s in range(far - 1, 0, -1):
        to_right = send((to_right.astype(jnp.float32) + for_right[s]).astype(jnp.bfloat16), right)
        to_left = send((to_left.astype(jnp.float32) + for_left[s]).astype(jnp.bfloat16), left)
    total = mine + to_right.astype(jnp.float32) + to_left.astype(jnp.float32)
    return total.astype(jnp.bfloat16)


def solution(mesh):
    cycle = chip_cycle(mesh.shape["expert"] // 2, mesh.shape["dp"])
    return jax.shard_map(
        functools.partial(on_device, cycle),
        mesh=mesh,
        in_specs=(
            P(("dp", "expert"), None),
            P(("dp", "expert"), None),
            P(("dp", "expert"), None),
            P("expert", None, None, None),
            P("expert", None, None, None),
            P("expert", None, None, None),
        ),
        out_specs=P(("dp", "expert"), None),
        check_vma=False,
    )
```

time: 326 us -> 160 us (0.49)
  the two profiles are of different devices: /device:TPU:13 before, /device:TPU:0 now
where the time goes in v1:
time: 160 us
  Pallas kernels  50.8 us (32%)
  waiting for transfers between devices  38 us (24%)
  blocking collectives  22 us (14%)
  between operations  20.8 us (13%)
  starting transfers between devices  18.1 us (11%)
  other arithmetic  5.57 us (3%)
  local copies, waits for them, and re-layouts  4.37 us (3%)
    pallas_call x4, Pallas kernels, ffn(): pl.pallas_call(ffn_kernel, grid=(4,), out_shape=jax.ShapeDtypeStruct((row...  50.8 us
    ppermute x19, waiting for transfers between devices, on_device(): send = lambda value, pairs: lax.ppermute(value, 'expert', pairs)  38 us
    all_gather x1, blocking collectives, on_device(): all_gates = lax.all_gather(dense.astype(jnp.bfloat16), 'expert')  22 us
    ppermute x19, starting transfers between devices, on_device(): send = lambda value, pairs: lax.ppermute(value, 'expert', pairs)  18.1 us
  transfers between devices with their start and end apart: 19, of which 6 were waited for; matrix products, arithmetic and copies ran while one was open for 5% of the time, Pallas kernels for 26%

profile of v1, /device:TPU:0, one launch (start us, length us, event | category | flops | bytes accessed | tf_op | source)
XLA Modules:
  0.0 159.7 jit_solution(3777769610313072220)
XLA Ops:
  0.0 0.5 collective-permute-start.2
  0.5 0.5 collective-permute-start.4
  1.0 2.6 %collective-permute-start = (bf16[128,2048]{1,0:T(8,128)(2,1)}, bf16[128,2048]{1,0:T(8,128)(2,1)S(1)}, u32[]{:S(2)}, u32[]{:S(2)}) collective-permute-start(bf16[128,2048]{1,0:T(8,128)(2,1)} %param.8), channel_id=1, source_target_pairs={{8,16},{10,18},{16,24},{18,26},{24,28},{26,30},{28,20},{30,22},{20... | collective-permute-start | bytes 1572872 | tf_op jit(solution)/shard_map/ppermute | solution.py:111
  3.5 12.7 %collective-permute-done = bf16[128,2048]{1,0:T(8,128)(2,1)S(1)} collective-permute-done((bf16[128,2048]{1,0:T(8,128)(2,1)}, bf16[128,2048]{1,0:T(8,128)(2,1)S(1)}, u32[]{:S(2)}, u32[]{:S(2)}) %collective-permute-start) | collective-permute-done | bytes 524320 | tf_op jit(solution)/shard_map/ppermute | solution.py:111
  16.3 1.8 %collective-permute-start.5 = (bf16[128,2048]{1,0:T(8,128)(2,1)S(1)}, bf16[128,2048]{1,0:T(8,128)(2,1)S(1)}, u32[]{:S(2)}, u32[]{:S(2)}) collective-permute-start(bf16[128,2048]{1,0:T(8,128)(2,1)S(1)} %collective-permute-done), channel_id=1, source_target_pairs={{8,16},{10,18},{16,24},{18,26},{24,28},{26,30},{28,20},{30,22},{20... | collective-permute-start | bytes 1572872 | tf_op jit(solution)/shard_map/ppermute | solution.py:111
  18.3 1.3 dynamic_slice.58
  25.3 1.6 %fusion.10 = (s32[1]{0:T(128)}, s32[1]{0:T(128)}, s32[1]{0:T(128)}, s32[1]{0:T(128)}, s32[1]{0:T(128)}, /*index=5*/s32[1]{0:T(128)}, s32[1]{0:T(128)}, s32[1]{0:T(128)}) fusion(s32[8]{0:T(128)} %constant.160.clone, s32[]{:T(128)S(6)} %select_n.128, s32[]{:T(128)S(6)} %select_n.134, s32[]{:T(128)S(6)} %select_n.131, s32[]{:T(128)S(6)} %select_n.125, ...), kind=kLoop, calls=%fused_computation.36 | loop fusion | bytes 96 | tf_op jit(solution)/shard_map/dynamic_slice | solution.py:128
  36.9 0.7 reduce_sum.18
  37.6 0.7 fusion.8
  38.3 0.7 select_reduce_fusion
  39.0 22.0 %all-gather = bf16[2048,16]{0,1:T(8,128)(2,1)S(1)} all-gather(bf16[128,16]{0,1:T(8,128)(2,1)S(1)} %select_reduce_fusion), channel_id=2, replica_groups=mesh['expert'=16,'dp'=2] {'expert'}, dimensions={0}, use_global_device_ids=true | all-gather | bytes 69632 | tf_op jit(solution)/shard_map/all_gather | solution.py:119
  66.3 2.0 %collective-permute-start.9 = (bf16[128,2048]{1,0:T(8,128)(2,1)S(1)}, bf16[128,2048]{1,0:T(8,128)(2,1)S(1)}, u32[]{:S(2)}, u32[]{:S(2)}) collective-permute-start(bf16[128,2048]{1,0:T(8,128)(2,1)S(1)} %collective-permute-done.8), channel_id=1, source_target_pairs={{8,0},{10,2},{16,8},{18,10},{24,16},{26,18},{28,24},{30,26},{20,28... | collective-permute-start | bytes 1572872 | tf_op jit(solution)/shard_map/ppermute | solution.py:111
  69.6 11.0 %collective-permute-done.9 = bf16[128,2048]{1,0:T(8,128)(2,1)S(1)} collective-permute-done((bf16[128,2048]{1,0:T(8,128)(2,1)S(1)}, bf16[128,2048]{1,0:T(8,128)(2,1)S(1)}, u32[]{:S(2)}, u32[]{:S(2)}) %collective-permute-start.9) | collective-permute-done | bytes 524320 | tf_op jit(solution)/shard_map/ppermute | solution.py:111
  80.6 1.7 %collective-permute-start.10 = (bf16[64,2048]{1,0:T(8,128)(2,1)S(1)}, bf16[64,2048]{1,0:T(8,128)(2,1)S(1)}, u32[]{:S(2)}, u32[]{:S(2)}) collective-permute-start(bf16[64,2048]{1,0:T(8,128)(2,1)S(1)} %slice.48), channel_id=1, source_target_pairs={{8,0},{10,2},{16,8},{18,10},{24,16},{26,18},{28,24},{30,26},{20,28... | collective-permute-start | bytes 786440 | tf_op jit(solution)/shard_map/ppermute | solution.py:111
  82.8 1.3 pad_maximum_fusion.x_ref
  84.2 4.2 %collective-permute-done.10 = bf16[64,2048]{1,0:T(8,128)(2,1)S(1)} collective-permute-done((bf16[64,2048]{1,0:T(8,128)(2,1)S(1)}, bf16[64,2048]{1,0:T(8,128)(2,1)S(1)}, u32[]{:S(2)}, u32[]{:S(2)}) %collective-permute-start.10) | collective-permute-done | bytes 262176 | tf_op jit(solution)/shard_map/ppermute | solution.py:111
  88.4 1.1 collective-permute-done.7
  89.6 9.6 %shard_map.83 = f32[128,2048]{1,0:T(8,128)S(1)} custom-call(bf16[128,2048]{1,0:T(8,128)(2,1)S(1)} %pad_maximum_fusion.3.x_ref, f32[128,2]{1,0:T(8,128)S(1)} %get-tuple-element.13.gate_ref, bf16[2,2048,384]{2,1,0:T(8,128)(2,1)S(1)} %bitcast.33, bf16[2,2048,384]{2,1,0:T(8,128)(2,1)} %bitcast.35, bf16[2,384,2048]{2,1,0:T(8,128)(2,1)} %bitcast.40, ...), custom_call_target="tpu_custom_call" | custom-call | flops 2415919104 | bytes 20447232 | tf_op jit(solution)/shard_map/pallas_call | solution.py:68
  99.3 0.7 collective-permute-start.11
  100.0 1.3 collective-permute-start.15
  101.4 12.7 %shard_map.84 = f32[256,2048]{1,0:T(8,128)S(1)} custom-call(bf16[256,2048]{1,0:T(8,128)(2,1)S(1)} %pad_maximum_fusion.1.x_ref, f32[256,2]{1,0:T(8,128)S(1)} %copy.30.gate_ref, bf16[2,2048,384]{2,1,0:T(8,128)(2,1)} %bitcast.30, bf16[2,2048,384]{2,1,0:T(8,128)(2,1)} %bitcast.36, bf16[2,384,2048]{2,1,0:T(8,128)(2,1)} %bitcast.41, ...), custom_call_target="tpu_custom_call" | custom-call | flops 4831838208 | bytes 22020096 | tf_op jit(solution)/shard_map/pallas_call | solution.py:68
  114.3 0.7 collective-permute-start.12
  115.0 1.4 collective-permute-start.16
  116.4 12.7 %shard_map.85 = f32[256,2048]{1,0:T(8,128)S(1)} custom-call(bf16[256,2048]{1,0:T(8,128)(2,1)S(1)} %pad_maximum_fusion.2.x_ref, f32[256,2]{1,0:T(8,128)S(1)} %copy.33.gate_ref, bf16[2,2048,384]{2,1,0:T(8,128)(2,1)} %bitcast.31, bf16[2,2048,384]{2,1,0:T(8,128)(2,1)} %bitcast.37, bf16[2,384,2048]{2,1,0:T(8,128)(2,1)} %bitcast.42, ...), custom_call_target="tpu_custom_call" | custom-call | flops 4831838208 | bytes 22020096 | tf_op jit(solution)/shard_map/pallas_call | solution.py:68
  129.4 0.7 collective-permute-start.13
  130.2 1.3 collective-permute-start.17
  131.5 15.9 %shard_map.82 = f32[384,2048]{1,0:T(8,128)S(1)} custom-call(bf16[384,2048]{1,0:T(8,128)(2,1)S(1)} %pad_maximum_fusion.x_ref, f32[384,2]{1,0:T(8,128)S(1)} %copy.27.gate_ref, bf16[2,2048,384]{2,1,0:T(8,128)(2,1)} %bitcast.32, bf16[2,2048,384]{2,1,0:T(8,128)(2,1)} %bitcast.38, bf16[2,384,2048]{2,1,0:T(8,128)(2,1)} %bitcast.43, ...), custom_call_target="tpu_custom_call" | custom-call | flops 7247757312 | bytes 23592960 | tf_op jit(solution)/shard_map/pallas_call | solution.py:68
  147.7 0.7 collective-permute-start.14
  148.5 1.3 collective-permute-start.18
  149.8 8.1 %collective-permute-done.14 = bf16[128,2048]{1,0:T(8,128)(2,1)S(1)} collective-permute-done((bf16[128,2048]{1,0:T(8,128)(2,1)S(1)}, bf16[128,2048]{1,0:T(8,128)(2,1)S(1)}, u32[]{:S(2)}, u32[]{:S(2)}) %collective-permute-start.14) | collective-permute-done | bytes 524320 | tf_op jit(solution)/shard_map/ppermute | solution.py:111
  158.0 0.7 collective-permute-done.18
  158.7 1.0 fusion.7
  (52 shorter events, 3.3 us)
Async XLA Ops:
  0.0 89.6 %collective-permute-start.2 = (bf16[2,2048,384]{2,1,0:T(8,128)(2,1)}, bf16[2,2048,384]{2,1,0:T(8,128)(2,1)}, u32[]{:S(2)}, u32[]{:S(2)}) collective-permute-start(bf16[2,2048,384]{2,1,0:T(8,128)(2,1)} %bitcast.29), channel_id=1, source_target_pairs={{0,2},{2,0},{4,6},{6,4},{8,10},{10,8},{12,14},{14,12},{16,18},{18,... | collective-permute-start | bytes 9437192 | tf_op jit(solution)/shard_map/ppermute | solution.py:111
  0.5 89.2 %collective-permute-start.3 = (bf16[2,2048,384]{2,1,0:T(8,128)(2,1)}, bf16[2,2048,384]{2,1,0:T(8,128)(2,1)}, u32[]{:S(2)}, u32[]{:S(2)}) collective-permute-start(bf16[2,2048,384]{2,1,0:T(8,128)(2,1)} %bitcast.34), channel_id=1, source_target_pairs={{0,2},{2,0},{4,6},{6,4},{8,10},{10,8},{12,14},{14,12},{16,18},{18,... | collective-permute-start | bytes 9437192 | tf_op jit(solution)/shard_map/ppermute | solution.py:111
  0.5 89.1 %collective-permute-start.4 = (bf16[2,384,2048]{2,1,0:T(8,128)(2,1)}, bf16[2,384,2048]{2,1,0:T(8,128)(2,1)}, u32[]{:S(2)}, u32[]{:S(2)}) collective-permute-start(bf16[2,384,2048]{2,1,0:T(8,128)(2,1)} %bitcast.39), channel_id=1, source_target_pairs={{0,2},{2,0},{4,6},{6,4},{8,10},{10,8},{12,14},{14,12},{16,18},{18,... | collective-permute-start | bytes 9437192 | tf_op jit(solution)/shard_map/ppermute | solution.py:111
  1.0 15.3 %collective-permute-start = (bf16[128,2048]{1,0:T(8,128)(2,1)}, bf16[128,2048]{1,0:T(8,128)(2,1)S(1)}, u32[]{:S(2)}, u32[]{:S(2)}) collective-permute-start(bf16[128,2048]{1,0:T(8,128)(2,1)} %param.8), channel_id=1, source_target_pairs={{8,16},{10,18},{16,24},{18,26},{24,28},{26,30},{28,20},{30,22},{20... | collective-permute-start | bytes 1572872 | tf_op jit(solution)/shard_map/ppermute | solution.py:111
  3.5 14.6 %collective-permute-start.1 = (bf16[128,2048]{1,0:T(8,128)(2,1)}, bf16[128,2048]{1,0:T(8,128)(2,1)S(1)}, u32[]{:S(2)}, u32[]{:S(2)}) collective-permute-start(bf16[128,2048]{1,0:T(8,128)(2,1)} %param.8), channel_id=1, source_target_pairs={{8,0},{10,2},{16,8},{18,10},{24,16},{26,18},{28,24},{30,26},{20,28... | collective-permute-start | bytes 1572872 | tf_op jit(solution)/shard_map/ppermute | solution.py:111
  16.3 50.0 %copy-start.2 = (bf16[128,2048]{1,0:T(8,128)(2,1)}, bf16[128,2048]{1,0:T(8,128)(2,1)S(1)}, u32[]{:S(2)}) copy-start(bf16[128,2048]{1,0:T(8,128)(2,1)S(1)} %collective-permute-done) | copy-start | bytes 1572868
  16.3 50.0 %collective-permute-start.5 = (bf16[128,2048]{1,0:T(8,128)(2,1)S(1)}, bf16[128,2048]{1,0:T(8,128)(2,1)S(1)}, u32[]{:S(2)}, u32[]{:S(2)}) collective-permute-start(bf16[128,2048]{1,0:T(8,128)(2,1)S(1)} %collective-permute-done), channel_id=1, source_target_pairs={{8,16},{10,18},{16,24},{18,26},{24,28},{26,30},{28,20},{30,22},{20... | collective-permute-start | bytes 1572872 | tf_op jit(solution)/shard_map/ppermute | solution.py:111
  18.1 48.2 %copy-start.3 = (bf16[128,2048]{1,0:T(8,128)(2,1)}, bf16[128,2048]{1,0:T(8,128)(2,1)S(1)}, u32[]{:S(2)}) copy-start(bf16[128,2048]{1,0:T(8,128)(2,1)S(1)} %collective-permute-done.1) | copy-start | bytes 1572868
  18.1 48.2 %collective-permute-start.8 = (bf16[128,2048]{1,0:T(8,128)(2,1)S(1)}, bf16[128,2048]{1,0:T(8,128)(2,1)S(1)}, u32[]{:S(2)}, u32[]{:S(2)}) collective-permute-start(bf16[128,2048]{1,0:T(8,128)(2,1)S(1)} %collective-permute-done.1), channel_id=1, source_target_pairs={{8,0},{10,2},{16,8},{18,10},{24,16},{26,18},{28,24},{30,26},{20,28... | collective-permute-start | bytes 1572872 | tf_op jit(solution)/shard_map/ppermute | solution.py:111
  61.0 21.7 %copy-start.1 = (bf16[128,2048]{1,0:T(8,128)(2,1)S(1)}, bf16[128,2048]{1,0:T(8,128)(2,1)}, u32[]{:S(2)}) copy-start(bf16[128,2048]{1,0:T(8,128)(2,1)} %param.8) | copy-start | bytes 1572868
  66.3 16.1 %collective-permute-start.6 = (bf16[128,2048]{1,0:T(8,128)(2,1)S(1)}, bf16[128,2048]{1,0:T(8,128)(2,1)S(1)}, u32[]{:S(2)}, u32[]{:S(2)}) collective-permute-start(bf16[128,2048]{1,0:T(8,128)(2,1)S(1)} %collective-permute-done.5), channel_id=1, source_target_pairs={{8,16},{10,18},{16,24},{18,26},{24,28},{26,30},{28,20},{30,22},{20... | collective-permute-start | bytes 1572872 | tf_op jit(solution)/shard_map/ppermute | solution.py:111
  66.3 14.2 %collective-permute-start.9 = (bf16[128,2048]{1,0:T(8,128)(2,1)S(1)}, bf16[128,2048]{1,0:T(8,128)(2,1)S(1)}, u32[]{:S(2)}, u32[]{:S(2)}) collective-permute-start(bf16[128,2048]{1,0:T(8,128)(2,1)S(1)} %collective-permute-done.8), channel_id=1, source_target_pairs={{8,0},{10,2},{16,8},{18,10},{24,16},{26,18},{28,24},{30,26},{20,28... | collective-permute-start | bytes 1572872 | tf_op jit(solution)/shard_map/ppermute | solution.py:111
  80.6 7.8 %collective-permute-start.10 = (bf16[64,2048]{1,0:T(8,128)(2,1)S(1)}, bf16[64,2048]{1,0:T(8,128)(2,1)S(1)}, u32[]{:S(2)}, u32[]{:S(2)}) collective-permute-start(bf16[64,2048]{1,0:T(8,128)(2,1)S(1)} %slice.48), channel_id=1, source_target_pairs={{8,0},{10,2},{16,8},{18,10},{24,16},{26,18},{28,24},{30,26},{20,28... | collective-permute-start | bytes 786440 | tf_op jit(solution)/shard_map/ppermute | solution.py:111
  82.3 7.2 %collective-permute-start.7 = (bf16[64,2048]{1,0:T(8,128)(2,1)S(1)}, bf16[64,2048]{1,0:T(8,128)(2,1)S(1)}, u32[]{:S(2)}, u32[]{:S(2)}) collective-permute-start(bf16[64,2048]{1,0:T(8,128)(2,1)S(1)} %slice.47), channel_id=1, source_target_pairs={{8,16},{10,18},{16,24},{18,26},{24,28},{26,30},{28,20},{30,22},{20... | collective-permute-start | bytes 786440 | tf_op jit(solution)/shard_map/ppermute | solution.py:111
  84.1 5.5 %copy-start = (bf16[1,2,2048,384]{3,2,1,0:T(8,128)(2,1)S(1)}, bf16[1,2,2048,384]{3,2,1,0:T(8,128)(2,1)}, u32[]{:S(2)}) copy-start(bf16[1,2,2048,384]{3,2,1,0:T(8,128)(2,1)} %param.11) | copy-start | bytes 9437188
  99.3 14.7 %collective-permute-start.11 = (bf16[64,2048]{1,0:T(8,128)(2,1)S(1)}, bf16[64,2048]{1,0:T(8,128)(2,1)S(1)}, u32[]{:S(2)}, u32[]{:S(2)}) collective-permute-start(bf16[64,2048]{1,0:T(8,128)(2,1)S(1)} %get-tuple-element.11), channel_id=1, source_target_pairs={{8,16},{10,18},{16,24},{18,26},{24,28},{26,30},{28,20},{30,22},{20... | collective-permute-start | bytes 786440 | tf_op jit(solution)/shard_map/ppermute | solution.py:111
  100.0 14.0 %collective-permute-start.15 = (bf16[64,2048]{1,0:T(8,128)(2,1)S(1)}, bf16[64,2048]{1,0:T(8,128)(2,1)S(1)}, u32[]{:S(2)}, u32[]{:S(2)}) collective-permute-start(bf16[64,2048]{1,0:T(8,128)(2,1)S(1)} %get-tuple-element.12), channel_id=1, source_target_pairs={{8,0},{10,2},{16,8},{18,10},{24,16},{26,18},{28,24},{30,26},{20,28... | collective-permute-start | bytes 786440 | tf_op jit(solution)/shard_map/ppermute | solution.py:111
  114.3 14.8 %collective-permute-start.12 = (bf16[128,2048]{1,0:T(8,128)(2,1)S(1)}, bf16[128,2048]{1,0:T(8,128)(2,1)S(1)}, u32[]{:S(2)}, u32[]{:S(2)}) collective-permute-start(bf16[128,2048]{1,0:T(8,128)(2,1)S(1)} %get-tuple-element.9), channel_id=1, source_target_pairs={{8,16},{10,18},{16,24},{18,26},{24,28},{26,30},{28,20},{30,22},{20... | collective-permute-start | bytes 1572872 | tf_op jit(solution)/shard_map/ppermute | solution.py:111
  115.0 14.1 %collective-permute-start.16 = (bf16[128,2048]{1,0:T(8,128)(2,1)S(1)}, bf16[128,2048]{1,0:T(8,128)(2,1)S(1)}, u32[]{:S(2)}, u32[]{:S(2)}) collective-permute-start(bf16[128,2048]{1,0:T(8,128)(2,1)S(1)} %get-tuple-element.10), channel_id=1, source_target_pairs={{8,0},{10,2},{16,8},{18,10},{24,16},{26,18},{28,24},{30,26},{20,28... | collective-permute-start | bytes 1572872 | tf_op jit(solution)/shard_map/ppermute | solution.py:111
  129.4 18.0 %collective-permute-start.13 = (bf16[128,2048]{1,0:T(8,128)(2,1)S(1)}, bf16[128,2048]{1,0:T(8,128)(2,1)S(1)}, u32[]{:S(2)}, u32[]{:S(2)}) collective-permute-start(bf16[128,2048]{1,0:T(8,128)(2,1)S(1)} %get-tuple-element.7), channel_id=1, source_target_pairs={{8,16},{10,18},{16,24},{18,26},{24,28},{26,30},{28,20},{30,22},{20... | collective-permute-start | bytes 1572872 | tf_op jit(solution)/shard_map/ppermute | solution.py:111
  130.2 17.3 %collective-permute-start.17 = (bf16[128,2048]{1,0:T(8,128)(2,1)S(1)}, bf16[128,2048]{1,0:T(8,128)(2,1)S(1)}, u32[]{:S(2)}, u32[]{:S(2)}) collective-permute-start(bf16[128,2048]{1,0:T(8,128)(2,1)S(1)} %get-tuple-element.8), channel_id=1, source_target_pairs={{8,0},{10,2},{16,8},{18,10},{24,16},{26,18},{28,24},{30,26},{20,28... | collective-permute-start | bytes 1572872 | tf_op jit(solution)/shard_map/ppermute | solution.py:111
  147.7 10.2 %collective-permute-start.14 = (bf16[128,2048]{1,0:T(8,128)(2,1)S(1)}, bf16[128,2048]{1,0:T(8,128)(2,1)S(1)}, u32[]{:S(2)}, u32[]{:S(2)}) collective-permute-start(bf16[128,2048]{1,0:T(8,128)(2,1)S(1)} %get-tuple-element.5), channel_id=1, source_target_pairs={{8,16},{10,18},{16,24},{18,26},{24,28},{26,30},{28,20},{30,22},{20... | collective-permute-start | bytes 1572872 | tf_op jit(solution)/shard_map/ppermute | solution.py:111
  148.5 10.2 %collective-permute-start.18 = (bf16[128,2048]{1,0:T(8,128)(2,1)S(1)}, bf16[128,2048]{1,0:T(8,128)(2,1)S(1)}, u32[]{:S(2)}, u32[]{:S(2)}) collective-permute-start(bf16[128,2048]{1,0:T(8,128)(2,1)S(1)} %get-tuple-element.6), channel_id=1, source_target_pairs={{8,0},{10,2},{16,8},{18,10},{24,16},{26,18},{28,24},{30,26},{20,28... | collective-permute-start | bytes 1572872 | tf_op jit(solution)/shard_map/ppermute | solution.py:111

commit v2 on v1

--- a/solution.py
+++ b/solution.py
@@ -19,10 +19,28 @@
     return walk + list(range(rows_n - 1, -1, -1))
 
 
-def ffn_kernel(x_ref, gate_ref, g0, u0, d0, g1, u1, d1, out_ref):
+def after(value, *earlier):
+    def kernel(value_ref, *refs):
+        refs[-1][...] = value_ref[...]
+
+    return pl.pallas_call(
+        kernel,
+        out_shape=jax.ShapeDtypeStruct(value.shape, value.dtype),
+        in_specs=[
+            pl.BlockSpec(memory_space=pltpu.VMEM),
+            *[pl.BlockSpec(memory_space=pl.ANY)] * len(earlier),
+        ],
+        out_specs=pl.BlockSpec(memory_space=pltpu.VMEM),
+    )(value, *earlier)
+
+
+def ffn_kernel(x_ref, gate_ref, g0, u0, d0, g1, u1, d1, earlier_ref, out_ref):
     i = pl.program_id(0)
     x = x_ref[...]
-    weight = jnp.where(i % 2 == 0, gate_ref[:, 0:1], gate_ref[:, 1:2])
+    expert = lax.axis_index("expert") // 2 * 2 + i % 2
+    lanes = lax.broadcasted_iota(jnp.int32, gate_ref.shape, 1)
+    gates = gate_ref[...].astype(jnp.float32)
+    weight = jnp.sum(jnp.where(lanes == expert, gates, 0.0), axis=1, keepdims=True)
 
     def add(g_ref, u_ref, d_ref, first):
         gate_h = jnp.dot(x, g_ref[0], preferred_element_type=jnp.float32)
@@ -53,7 +71,7 @@
         add(g1, u1, d1, False)
 
 
-def ffn(x, gates, own, other):
+def ffn(x, gates, own, other, earlier):
     rows, width = x.shape
     half = own[0].shape[2]
 
@@ -71,34 +89,29 @@
         out_shape=jax.ShapeDtypeStruct((rows, width), jnp.float32),
         in_specs=[
             pl.BlockSpec((rows, width), lambda i: (0, 0)),
-            pl.BlockSpec((rows, 2), lambda i: (0, 0)),
+            pl.BlockSpec((rows, gates.shape[1]), lambda i: (0, 0)),
             early((width, half)),
             early((width, half)),
             early((half, width)),
             late((width, half)),
             late((width, half)),
             late((half, width)),
+            pl.BlockSpec(memory_space=pl.ANY),
         ],
         out_specs=pl.BlockSpec((rows, width), lambda i: (0, 0)),
         cost_estimate=pl.CostEstimate(
             flops=flops, bytes_accessed=moved, transcendentals=4 * rows * half
         ),
         compiler_params=pltpu.CompilerParams(vmem_limit_bytes=48 * 2**20),
-    )(x, gates, *own, *other)
+    )(x, gates, *own, *other, earlier)
 
 
 def on_device(cycle, tokens, expert_ids, route_weight, w_gate, w_up, w_down):
     devices_n = lax.axis_size("expert")
-    index = lax.axis_index("expert")
     chips_n = devices_n // 2
-    chip, core = index // 2, index % 2
     rows = tokens.shape[0]
     cut = rows // 2
     far = chips_n // 2
-    place = [0] * chips_n
-    for i, c in enumerate(cycle):
-        place[c] = i
-
     def turn(step):
         pairs = []
         for i, c in enumerate(cycle):
@@ -116,44 +129,46 @@
 
     own = (w_gate[0], w_up[0], w_down[0])
     other = tuple(send(w, swap) for w in own)
-    all_gates = lax.all_gather(dense.astype(jnp.bfloat16), "expert")
-    all_gates = all_gates.reshape(chips_n, 2, rows, devices_n)
-    all_gates = lax.dynamic_index_in_dim(all_gates, core, 1, keepdims=False)
-    all_gates = lax.dynamic_slice_in_dim(all_gates, 2 * chip, 2, 2).astype(jnp.float32)
-    here = jnp.array(place, jnp.int32)[chip]
-    walk = jnp.array(cycle, jnp.int32)
-
-    def gates_at(distance):
-        return lax.dynamic_index_in_dim(
-            all_gates, walk[(here + distance + chips_n) % chips_n], 0, keepdims=False
-        )
-
     from_left, from_right = {0: tokens}, {0: tokens}
     for s in range(1, far):
-        from_left[s] = send(from_left[s - 1], right)
-        from_right[s] = send(from_right[s - 1], left)
+        on_right, on_left = from_left[s - 1], from_right[s - 1]
+        if s == min(3, far - 1):
+            on_right, on_left = after(on_right, *other), after(on_left, *other)
+        from_left[s] = send(on_right, right)
+        from_right[s] = send(on_left, left)
+    dense = dense.astype(jnp.bfloat16)
+    sooner = after(dense, from_left[1])
+    gates_at = {0: dense, -1: send(sooner, turn(1)), 1: send(sooner, turn(-1))}
+
+    def outputs(blocks, distances, earlier):
+        x = jnp.concatenate(blocks) if len(blocks) > 1 else blocks[0]
+        g = jnp.concatenate([gates_at[d] for d in distances])
+        return ffn(x, g, own, other, earlier)
+
+    near = outputs([from_left[1], from_right[1]], [-1, 1], from_left[min(2, far - 1)])
+    later = after(dense, near)
+    for s in range(2, far):
+        gates_at[-s], gates_at[s] = send(later, turn(s)), send(later, turn(-s))
+    gates_at[far] = send(later, turn(far))
     far_block = jnp.concatenate(
-        [send(from_left[far - 1][:cut], right), send(from_right[far - 1][cut:], left)]
+        [
+            send(after(from_left[far - 1][:cut], near), right),
+            send(after(from_right[far - 1][cut:], near), left),
+        ]
     )
-
-    def outputs(blocks, distances):
-        x = jnp.concatenate(blocks) if len(blocks) > 1 else blocks[0]
-        g = jnp.concatenate([gates_at(d) for d in distances])
-        return ffn(x, g, own, other)
-
-    near = outputs([from_left[1], from_right[1], tokens], [-1, 1, 0])
-    for_left, for_right = {1: near[:rows]}, {1: near[rows : 2 * rows]}
-    mine = near[2 * rows :]
+    last = outputs([far_block], [far], near)
+    for_left, for_right = {1: near[:rows]}, {1: near[rows:]}
     for s in range(2, far):
-        both = outputs([from_left[s], from_right[s]], [-s, s])
+        both = outputs([from_left[s], from_right[s]], [-s, s], last)
         for_left[s], for_right[s] = both[:rows], both[rows:]
-    last = outputs([far_block], [far])
 
     to_right = send(last[:cut].astype(jnp.bfloat16), right)
     to_left = send(last[cut:].astype(jnp.bfloat16), left)
     to_right = jnp.pad(to_right, ((0, cut), (0, 0)))
     to_left = jnp.pad(to_left, ((cut, 0), (0, 0)))
     for s in range(far - 1, 0, -1):
+        if s == 1:
+            mine = outputs([tokens], [0], to_right)
         to_right = send((to_right.astype(jnp.float32) + for_right[s]).astype(jnp.bfloat16), right)
         to_left = send((to_left.astype(jnp.float32) + for_left[s]).astype(jnp.bfloat16), left)
     total = mine + to_right.astype(jnp.float32) + to_left.astype(jnp.float32)

time: 160 us -> 149 us (0.931)
  blocking collectives: 22 us -> 0 us
  between operations: 20.8 us -> 0.28 us
  Pallas kernels: 50.8 us -> 67.7 us
  starting transfers between devices: 18.1 us -> 31.6 us
    all_gather x1 -> x0, blocking collectives: 22 us -> none  [on_device(): all_gates = lax.all_gather(dense.astype(jnp.bfloat16), 'expert')]
    ppermute x19 -> x26, starting transfers between devices: 18.1 us -> 31.6 us  [on_device(): send = lambda value, pairs: lax.ppermute(value, 'expert', pairs)]
    pallas_call x0 -> x6, Pallas kernels: none -> 9.89 us  [after(): pl.pallas_call(kernel, out_shape=jax.ShapeDtypeStruct(value.shape, value....]
    pallas_call x4 -> x5, Pallas kernels: 50.8 us -> 57.8 us  [ffn(): pl.pallas_call(ffn_kernel, grid=(4,), out_shape=jax.ShapeDtypeStruct((row...]
    unnamed x8 -> x24, local copies, waits for them, and re-layouts: 0.02 us -> 3.74 us
    dynamic_slice x9 -> x0, local copies, waits for them, and re-layouts: 3.47 us -> none  [the longest x1 1.65 us: gates_at(): walk[(here + distance + chips_n) % chips_n]]
    ppermute x19 -> x26, waiting for transfers between devices: 38 us -> 37.8 us  [on_device(): send = lambda value, pairs: lax.ppermute(value, 'expert', pairs)]
  transfers between devices with their start and end apart: 19 -> 26, of which waited for: 6 -> 7; matrix products, arithmetic and copies ran while one was open for 5% -> 4% of each run, Pallas kernels for 26% -> 46%
where the time goes in v2:
time: 149 us
  Pallas kernels  67.7 us (45%)
  waiting for transfers between devices  37.8 us (25%)
  starting transfers between devices  31.6 us (21%)
  local copies, waits for them, and re-layouts  5.94 us (4%)
  other arithmetic  5.28 us (4%)
    pallas_call x5, Pallas kernels, ffn(): pl.pallas_call(ffn_kernel, grid=(4,), out_shape=jax.ShapeDtypeStruct((row...  57.8 us
    ppermute x26, waiting for transfers between devices, on_device(): send = lambda value, pairs: lax.ppermute(value, 'expert', pairs)  37.8 us
    ppermute x26, starting transfers between devices, on_device(): send = lambda value, pairs: lax.ppermute(value, 'expert', pairs)  31.6 us
    pallas_call x6, Pallas kernels, after(): pl.pallas_call(kernel, out_shape=jax.ShapeDtypeStruct(value.shape, value....  9.89 us
    unnamed x24, local copies, waits for them, and re-layouts  3.74 us
  transfers between devices with their start and end apart: 26, of which 7 were waited for; matrix products, arithmetic and copies ran while one was open for 4% of the time, Pallas kernels for 46%

profile of v2, /device:TPU:0, one launch (start us, length us, event | category | flops | bytes accessed | tf_op | source)
XLA Modules:
  0.0 148.6 jit_solution(637603894341503512)
XLA Ops:
  1.0 2.6 %collective-permute-start.3 = (bf16[128,2048]{1,0:T(8,128)(2,1)}, bf16[128,2048]{1,0:T(8,128)(2,1)S(1)}, u32[]{:S(2)}, u32[]{:S(2)}) collective-permute-start(bf16[128,2048]{1,0:T(8,128)(2,1)} %x_ref.1), channel_id=1, source_target_pairs={{8,16},{10,18},{16,24},{18,26},{24,28},{26,30},{28,20},{30,22},{20... | collective-permute-start | bytes 1572872 | tf_op jit(solution)/shard_map/ppermute | solution.py:124
  6.4 9.9 %collective-permute-done.3.refs_0_ = bf16[128,2048]{1,0:T(8,128)(2,1)S(1)} collective-permute-done((bf16[128,2048]{1,0:T(8,128)(2,1)}, bf16[128,2048]{1,0:T(8,128)(2,1)S(1)}, u32[]{:S(2)}, u32[]{:S(2)}) %collective-permute-start.3) | collective-permute-done | bytes 524320 | tf_op jit(solution)/shard_map/ppermute | solution.py:124
  17.1 1.4 shard_map.65
  18.5 1.8 %collective-permute-start.7 = (bf16[128,16]{1,0:T(8,128)(2,1)}, bf16[128,16]{1,0:T(8,128)(2,1)S(1)}, u32[]{:S(2)}, u32[]{:S(2)}) collective-permute-start(bf16[128,16]{1,0:T(8,128)(2,1)} %shard_map.65), channel_id=1, source_target_pairs={{8,16},{10,18},{16,24},{18,26},{24,28},{26,30},{28,20},{30,22},{20... | collective-permute-start | bytes 12296 | tf_op jit(solution)/shard_map/ppermute | solution.py:124
  20.5 2.1 %collective-permute-done.7 = bf16[128,16]{1,0:T(8,128)(2,1)S(1)} collective-permute-done((bf16[128,16]{1,0:T(8,128)(2,1)}, bf16[128,16]{1,0:T(8,128)(2,1)S(1)}, u32[]{:S(2)}, u32[]{:S(2)}) %collective-permute-start.7) | collective-permute-done | bytes 4128 | tf_op jit(solution)/shard_map/ppermute | solution.py:124
  22.6 1.8 %collective-permute-start.4 = (bf16[128,2048]{1,0:T(8,128)(2,1)}, bf16[128,2048]{1,0:T(8,128)(2,1)S(1)}, u32[]{:S(2)}, u32[]{:S(2)}) collective-permute-start(bf16[128,2048]{1,0:T(8,128)(2,1)} %copy-done.9), channel_id=1, source_target_pairs={{8,16},{10,18},{16,24},{18,26},{24,28},{26,30},{28,20},{30,22},{20... | collective-permute-start | bytes 1572872 | tf_op jit(solution)/shard_map/ppermute | solution.py:124
  24.6 1.1 pad_maximum_fusion.x_ref
  25.8 9.6 %collective-permute-done.4.value_ref.earlier_ref = bf16[128,2048]{1,0:T(8,128)(2,1)S(1)} collective-permute-done((bf16[128,2048]{1,0:T(8,128)(2,1)}, bf16[128,2048]{1,0:T(8,128)(2,1)S(1)}, u32[]{:S(2)}, u32[]{:S(2)}) %collective-permute-start.4) | collective-permute-done | bytes 524320 | tf_op jit(solution)/shard_map/ppermute | solution.py:124
  36.2 1.9 %shard_map.64 = bf16[128,2048]{1,0:T(8,128)(2,1)} custom-call(bf16[128,2048]{1,0:T(8,128)(2,1)} %copy-done.3, bf16[2,2048,384]{2,1,0:T(8,128)(2,1)} %collective-permute-done.refs_0_.g1, bf16[2,2048,384]{2,1,0:T(8,128)(2,1)} %collective-permute-done.1.refs_1_.u1, bf16[2,384,2048]{2,1,0:T(8,128)(2,1)} %collective-permute-done.2.refs_2_.d1), custom_call_target="tpu_custom_call" | custom-call | tf_op jit(solution)/shard_map/pallas_call | solution.py:26
  38.1 1.6 %collective-permute-start.5 = (bf16[128,2048]{1,0:T(8,128)(2,1)}, bf16[128,2048]{1,0:T(8,128)(2,1)S(1)}, u32[]{:S(2)}, u32[]{:S(2)}) collective-permute-start(bf16[128,2048]{1,0:T(8,128)(2,1)} %shard_map.64), channel_id=1, source_target_pairs={{8,16},{10,18},{16,24},{18,26},{24,28},{26,30},{28,20},{30,22},{20... | collective-permute-start | bytes 1572872 | tf_op jit(solution)/shard_map/ppermute | solution.py:124
  40.5 1.9 %shard_map.68 = bf16[128,2048]{1,0:T(8,128)(2,1)} custom-call(bf16[128,2048]{1,0:T(8,128)(2,1)} %copy-done.7, bf16[2,2048,384]{2,1,0:T(8,128)(2,1)} %collective-permute-done.refs_0_.g1, bf16[2,2048,384]{2,1,0:T(8,128)(2,1)} %collective-permute-done.1.refs_1_.u1, bf16[2,384,2048]{2,1,0:T(8,128)(2,1)} %collective-permute-done.2.refs_2_.d1), custom_call_target="tpu_custom_call" | custom-call | tf_op jit(solution)/shard_map/pallas_call | solution.py:26
  42.8 12.7 %shard_map.66.refs_0_.earlier_ref = f32[256,2048]{1,0:T(8,128)S(1)} custom-call(bf16[256,2048]{1,0:T(8,128)(2,1)S(1)} %pad_maximum_fusion.x_ref, bf16[256,16]{1,0:T(8,128)(2,1)S(1)} %pad_maximum_fusion.4.gate_ref, bf16[2,2048,384]{2,1,0:T(8,128)(2,1)} %bitcast.4, bf16[2,2048,384]{2,1,0:T(8,128)(2,1)} %bitcast.10, bf16[2,384,2048]{2,1,0:T(8,128)(2,1)} %bitcast.16, ...), custom_call_target="tpu_custom_call" | custom-call | flops 4831838208 | bytes 22020096 | tf_op jit(solution)/shard_map/pallas_call | solution.py:86
  55.5 1.3 copy-done.1
  56.8 1.4 shard_map.70
  58.3 3.6 %collective-permute-start.15 = (bf16[128,16]{1,0:T(8,128)(2,1)}, bf16[128,16]{1,0:T(8,128)(2,1)S(1)}, u32[]{:S(2)}, u32[]{:S(2)}) collective-permute-start(bf16[128,16]{1,0:T(8,128)(2,1)} %shard_map.70), channel_id=1, source_target_pairs={{8,28},{10,30},{16,20},{18,22},{24,12},{26,14},{28,4},{30,6},{20,0... | collective-permute-start | bytes 12296 | tf_op jit(solution)/shard_map/ppermute | solution.py:124
  62.2 4.6 %collective-permute-start.13 = (bf16[128,16]{1,0:T(8,128)(2,1)S(1)}, bf16[128,16]{1,0:T(8,128)(2,1)S(1)}, u32[]{:S(2)}, u32[]{:S(2)}) collective-permute-start(bf16[128,16]{1,0:T(8,128)(2,1)S(1)} %copy-done.11), channel_id=1, source_target_pairs={{8,20},{10,22},{16,12},{18,14},{24,4},{26,6},{28,0},{30,2},{20,8},... | collective-permute-start | bytes 12296 | tf_op jit(solution)/shard_map/ppermute | solution.py:124
  67.6 1.7 %shard_map.67 = bf16[64,2048]{1,0:T(8,128)(2,1)} custom-call(bf16[64,2048]{1,0:T(8,128)(2,1)} %slice.42.value_ref, f32[256,2048]{1,0:T(8,128)} %copy-done.1), custom_call_target="tpu_custom_call" | custom-call | tf_op jit(solution)/shard_map/pallas_call | solution.py:26
  69.3 2.9 %collective-permute-start.19 = (bf16[128,16]{1,0:T(8,128)(2,1)S(1)}, bf16[128,16]{1,0:T(8,128)(2,1)S(1)}, u32[]{:S(2)}, u32[]{:S(2)}) collective-permute-start(bf16[128,16]{1,0:T(8,128)(2,1)S(1)} %copy-done.11), channel_id=1, source_target_pairs={{8,4},{10,6},{16,0},{18,2},{24,8},{26,10},{28,16},{30,18},{20,24},... | collective-permute-start | bytes 12296 | tf_op jit(solution)/shard_map/ppermute | solution.py:124
  72.9 1.7 %shard_map.69 = bf16[64,2048]{1,0:T(8,128)(2,1)} custom-call(bf16[64,2048]{1,0:T(8,128)(2,1)} %slice.43.value_ref, f32[256,2048]{1,0:T(8,128)} %copy-done.1), custom_call_target="tpu_custom_call" | custom-call | tf_op jit(solution)/shard_map/pallas_call | solution.py:26
  74.7 2.0 %collective-permute-start.12 = (bf16[64,2048]{1,0:T(8,128)(2,1)}, bf16[64,2048]{1,0:T(8,128)(2,1)S(1)}, u32[]{:S(2)}, u32[]{:S(2)}) collective-permute-start(bf16[64,2048]{1,0:T(8,128)(2,1)} %shard_map.69), channel_id=1, source_target_pairs={{8,0},{10,2},{16,8},{18,10},{24,16},{26,18},{28,24},{30,26},{20,28... | collective-permute-start | bytes 786440 | tf_op jit(solution)/shard_map/ppermute | solution.py:124
  76.8 4.2 %collective-permute-done.9 = bf16[64,2048]{1,0:T(8,128)(2,1)S(1)} collective-permute-done((bf16[64,2048]{1,0:T(8,128)(2,1)S(1)}, bf16[64,2048]{1,0:T(8,128)(2,1)S(1)}, u32[]{:S(2)}, u32[]{:S(2)}) %collective-permute-start.9) | collective-permute-done | bytes 262176 | tf_op jit(solution)/shard_map/ppermute | solution.py:124
  81.4 10.1 %shard_map.71.earlier_ref = f32[128,2048]{1,0:T(8,128)S(1)} custom-call(bf16[128,2048]{1,0:T(8,128)(2,1)S(1)} %pad_maximum_fusion.3.x_ref, bf16[128,16]{1,0:T(8,128)(2,1)S(1)} %collective-permute-done.13.gate_ref, bf16[2,2048,384]{2,1,0:T(8,128)(2,1)} %bitcast.5, bf16[2,2048,384]{2,1,0:T(8,128)(2,1)} %bitcast.11, bf16[2,384,2048]{2,1,0:T(8,128)(2,1)} %bitcast.17, ...), custom_call_target="tpu_custom_call" | custom-call | flops 2415919104 | bytes 20447232 | tf_op jit(solution)/shard_map/pallas_call | solution.py:86
  92.1 1.7 %collective-permute-start.22 = (bf16[64,2048]{1,0:T(8,128)(2,1)S(1)}, bf16[64,2048]{1,0:T(8,128)(2,1)S(1)}, u32[]{:S(2)}, u32[]{:S(2)}) collective-permute-start(bf16[64,2048]{1,0:T(8,128)(2,1)S(1)} %get-tuple-element.12), channel_id=1, source_target_pairs={{8,0},{10,2},{16,8},{18,10},{24,16},{26,18},{28,24},{30,26},{20,28... | collective-permute-start | bytes 786440 | tf_op jit(solution)/shard_map/ppermute | solution.py:124
  93.8 12.7 %shard_map.72 = f32[256,2048]{1,0:T(8,128)S(1)} custom-call(bf16[256,2048]{1,0:T(8,128)(2,1)S(1)} %pad_maximum_fusion.1.x_ref, bf16[256,16]{1,0:T(8,128)(2,1)S(1)} %pad_maximum_fusion.5.gate_ref, bf16[2,2048,384]{2,1,0:T(8,128)(2,1)} %bitcast.6, bf16[2,2048,384]{2,1,0:T(8,128)(2,1)} %bitcast.12, bf16[2,384,2048]{2,1,0:T(8,128)(2,1)} %bitcast.18, ...), custom_call_target="tpu_custom_call" | custom-call | flops 4831838208 | bytes 22020096 | tf_op jit(solution)/shard_map/pallas_call | solution.py:86
  107.1 1.7 %collective-permute-start.23 = (bf16[128,2048]{1,0:T(8,128)(2,1)S(1)}, bf16[128,2048]{1,0:T(8,128)(2,1)S(1)}, u32[]{:S(2)}, u32[]{:S(2)}) collective-permute-start(bf16[128,2048]{1,0:T(8,128)(2,1)S(1)} %get-tuple-element.10), channel_id=1, source_target_pairs={{8,0},{10,2},{16,8},{18,10},{24,16},{26,18},{28,24},{30,26},{20,28... | collective-permute-start | bytes 1572872 | tf_op jit(solution)/shard_map/ppermute | solution.py:124
  108.8 12.7 %shard_map.73 = f32[256,2048]{1,0:T(8,128)S(1)} custom-call(bf16[256,2048]{1,0:T(8,128)(2,1)S(1)} %pad_maximum_fusion.2.x_ref, bf16[256,16]{1,0:T(8,128)(2,1)S(1)} %pad_maximum_fusion.6.gate_ref, bf16[2,2048,384]{2,1,0:T(8,128)(2,1)} %bitcast.7, bf16[2,2048,384]{2,1,0:T(8,128)(2,1)} %bitcast.13, bf16[2,384,2048]{2,1,0:T(8,128)(2,1)} %bitcast.19, ...), custom_call_target="tpu_custom_call" | custom-call | flops 4831838208 | bytes 22020096 | tf_op jit(solution)/shard_map/pallas_call | solution.py:86
  122.3 1.7 %collective-permute-start.24 = (bf16[128,2048]{1,0:T(8,128)(2,1)S(1)}, bf16[128,2048]{1,0:T(8,128)(2,1)S(1)}, u32[]{:S(2)}, u32[]{:S(2)}) collective-permute-start(bf16[128,2048]{1,0:T(8,128)(2,1)S(1)} %get-tuple-element.8), channel_id=1, source_target_pairs={{8,0},{10,2},{16,8},{18,10},{24,16},{26,18},{28,24},{30,26},{20,28... | collective-permute-start | bytes 1572872 | tf_op jit(solution)/shard_map/ppermute | solution.py:124
  124.0 11.1 %collective-permute-done.20.earlier_ref = bf16[128,2048]{1,0:T(8,128)(2,1)S(1)} collective-permute-done((bf16[128,2048]{1,0:T(8,128)(2,1)S(1)}, bf16[128,2048]{1,0:T(8,128)(2,1)S(1)}, u32[]{:S(2)}, u32[]{:S(2)}) %collective-permute-start.20) | collective-permute-done | bytes 524320 | tf_op jit(solution)/shard_map/ppermute | solution.py:124
  135.8 1.3 collective-permute-start.21
  137.1 0.9 collective-permute-start.25
  137.9 9.6 %shard_map.74 = f32[128,2048]{1,0:T(8,128)S(1)} custom-call(bf16[128,2048]{1,0:T(8,128)(2,1)S(1)} %copy-done.6, bf16[128,16]{1,0:T(8,128)(2,1)S(1)} %copy-done.5, bf16[2,2048,384]{2,1,0:T(8,128)(2,1)S(1)} %bitcast.8, bf16[2,2048,384]{2,1,0:T(8,128)(2,1)} %bitcast.14, bf16[2,384,2048]{2,1,0:T(8,128)(2,1)} %bitcast.20, ...), custom_call_target="tpu_custom_call" | custom-call | flops 2415919104 | bytes 20447232 | tf_op jit(solution)/shard_map/pallas_call | solution.py:86
  147.6 1.0 add_convert_fusion
  (74 shorter events, 12.0 us)
Async XLA Ops:
  0.0 35.4 %collective-permute-start = (bf16[2,2048,384]{2,1,0:T(8,128)(2,1)}, bf16[2,2048,384]{2,1,0:T(8,128)(2,1)}, u32[]{:S(2)}, u32[]{:S(2)}) collective-permute-start(bf16[2,2048,384]{2,1,0:T(8,128)(2,1)} %bitcast.3), channel_id=1, source_target_pairs={{0,2},{2,0},{4,6},{6,4},{8,10},{10,8},{12,14},{14,12},{16,18},{18,... | collective-permute-start | bytes 9437192 | tf_op jit(solution)/shard_map/ppermute | solution.py:124
  0.5 35.0 %collective-permute-start.1 = (bf16[2,2048,384]{2,1,0:T(8,128)(2,1)}, bf16[2,2048,384]{2,1,0:T(8,128)(2,1)}, u32[]{:S(2)}, u32[]{:S(2)}) collective-permute-start(bf16[2,2048,384]{2,1,0:T(8,128)(2,1)} %bitcast.9), channel_id=1, source_target_pairs={{0,2},{2,0},{4,6},{6,4},{8,10},{10,8},{12,14},{14,12},{16,18},{18,... | collective-permute-start | bytes 9437192 | tf_op jit(solution)/shard_map/ppermute | solution.py:124
  0.5 34.9 %collective-permute-start.2 = (bf16[2,384,2048]{2,1,0:T(8,128)(2,1)}, bf16[2,384,2048]{2,1,0:T(8,128)(2,1)}, u32[]{:S(2)}, u32[]{:S(2)}) collective-permute-start(bf16[2,384,2048]{2,1,0:T(8,128)(2,1)} %bitcast.15), channel_id=1, source_target_pairs={{0,2},{2,0},{4,6},{6,4},{8,10},{10,8},{12,14},{14,12},{16,18},{18,... | collective-permute-start | bytes 9437192 | tf_op jit(solution)/shard_map/ppermute | solution.py:124
  1.0 15.3 %collective-permute-start.3 = (bf16[128,2048]{1,0:T(8,128)(2,1)}, bf16[128,2048]{1,0:T(8,128)(2,1)S(1)}, u32[]{:S(2)}, u32[]{:S(2)}) collective-permute-start(bf16[128,2048]{1,0:T(8,128)(2,1)} %x_ref.1), channel_id=1, source_target_pairs={{8,16},{10,18},{16,24},{18,26},{24,28},{26,30},{28,20},{30,22},{20... | collective-permute-start | bytes 1572872 | tf_op jit(solution)/shard_map/ppermute | solution.py:124
  3.5 16.7 %collective-permute-start.6 = (bf16[128,2048]{1,0:T(8,128)(2,1)}, bf16[128,2048]{1,0:T(8,128)(2,1)S(1)}, u32[]{:S(2)}, u32[]{:S(2)}) collective-permute-start(bf16[128,2048]{1,0:T(8,128)(2,1)} %x_ref.1), channel_id=1, source_target_pairs={{8,0},{10,2},{16,8},{18,10},{24,16},{26,18},{28,24},{30,26},{20,28... | collective-permute-start | bytes 1572872 | tf_op jit(solution)/shard_map/ppermute | solution.py:124
  18.5 4.1 %collective-permute-start.7 = (bf16[128,16]{1,0:T(8,128)(2,1)}, bf16[128,16]{1,0:T(8,128)(2,1)S(1)}, u32[]{:S(2)}, u32[]{:S(2)}) collective-permute-start(bf16[128,16]{1,0:T(8,128)(2,1)} %shard_map.65), channel_id=1, source_target_pairs={{8,16},{10,18},{16,24},{18,26},{24,28},{26,30},{28,20},{30,22},{20... | collective-permute-start | bytes 12296 | tf_op jit(solution)/shard_map/ppermute | solution.py:124
  20.3 4.1 %collective-permute-start.8 = (bf16[128,16]{1,0:T(8,128)(2,1)}, bf16[128,16]{1,0:T(8,128)(2,1)S(1)}, u32[]{:S(2)}, u32[]{:S(2)}) collective-permute-start(bf16[128,16]{1,0:T(8,128)(2,1)} %shard_map.65), channel_id=1, source_target_pairs={{8,0},{10,2},{16,8},{18,10},{24,16},{26,18},{28,24},{30,26},{20,28... | collective-permute-start | bytes 12296 | tf_op jit(solution)/shard_map/ppermute | solution.py:124
  22.6 12.8 %collective-permute-start.4 = (bf16[128,2048]{1,0:T(8,128)(2,1)}, bf16[128,2048]{1,0:T(8,128)(2,1)S(1)}, u32[]{:S(2)}, u32[]{:S(2)}) collective-permute-start(bf16[128,2048]{1,0:T(8,128)(2,1)} %copy-done.9), channel_id=1, source_target_pairs={{8,16},{10,18},{16,24},{18,26},{24,28},{26,30},{28,20},{30,22},{20... | collective-permute-start | bytes 1572872 | tf_op jit(solution)/shard_map/ppermute | solution.py:124
  24.4 15.3 %collective-permute-start.10 = (bf16[128,2048]{1,0:T(8,128)(2,1)S(1)}, bf16[128,2048]{1,0:T(8,128)(2,1)S(1)}, u32[]{:S(2)}, u32[]{:S(2)}) collective-permute-start(bf16[128,2048]{1,0:T(8,128)(2,1)S(1)} %collective-permute-done.6), channel_id=1, source_target_pairs={{8,0},{10,2},{16,8},{18,10},{24,16},{26,18},{28,24},{30,26},{20,28... | collective-permute-start | bytes 1572872 | tf_op jit(solution)/shard_map/ppermute | solution.py:124
  38.1 28.8 %collective-permute-start.5 = (bf16[128,2048]{1,0:T(8,128)(2,1)}, bf16[128,2048]{1,0:T(8,128)(2,1)S(1)}, u32[]{:S(2)}, u32[]{:S(2)}) collective-permute-start(bf16[128,2048]{1,0:T(8,128)(2,1)} %shard_map.64), channel_id=1, source_target_pairs={{8,16},{10,18},{16,24},{18,26},{24,28},{26,30},{28,20},{30,22},{20... | collective-permute-start | bytes 1572872 | tf_op jit(solution)/shard_map/ppermute | solution.py:124
  42.4 26.9 %collective-permute-start.11 = (bf16[128,2048]{1,0:T(8,128)(2,1)}, bf16[128,2048]{1,0:T(8,128)(2,1)S(1)}, u32[]{:S(2)}, u32[]{:S(2)}) collective-permute-start(bf16[128,2048]{1,0:T(8,128)(2,1)} %shard_map.68), channel_id=1, source_target_pairs={{8,0},{10,2},{16,8},{18,10},{24,16},{26,18},{28,24},{30,26},{20,28... | collective-permute-start | bytes 1572872 | tf_op jit(solution)/shard_map/ppermute | solution.py:124
  56.8 5.3 %copy-start.8 = (bf16[128,2048]{1,0:T(8,128)(2,1)S(1)}, bf16[128,2048]{1,0:T(8,128)(2,1)}, u32[]{:S(2)}) copy-start(bf16[128,2048]{1,0:T(8,128)(2,1)} %copy-done.7) | copy-start | bytes 1572868
  58.3 16.3 %collective-permute-start.15 = (bf16[128,16]{1,0:T(8,128)(2,1)}, bf16[128,16]{1,0:T(8,128)(2,1)S(1)}, u32[]{:S(2)}, u32[]{:S(2)}) collective-permute-start(bf16[128,16]{1,0:T(8,128)(2,1)} %shard_map.70), channel_id=1, source_target_pairs={{8,28},{10,30},{16,20},{18,22},{24,12},{26,14},{28,4},{30,6},{20,0... | collective-permute-start | bytes 12296 | tf_op jit(solution)/shard_map/ppermute | solution.py:124
  61.9 12.8 %collective-permute-start.16 = (bf16[128,16]{1,0:T(8,128)(2,1)}, bf16[128,16]{1,0:T(8,128)(2,1)S(1)}, u32[]{:S(2)}, u32[]{:S(2)}) collective-permute-start(bf16[128,16]{1,0:T(8,128)(2,1)} %shard_map.70), channel_id=1, source_target_pairs={{8,12},{10,14},{16,4},{18,6},{24,0},{26,2},{28,8},{30,10},{20,16},... | collective-permute-start | bytes 12296 | tf_op jit(solution)/shard_map/ppermute | solution.py:124
  62.2 19.1 %collective-permute-start.13 = (bf16[128,16]{1,0:T(8,128)(2,1)S(1)}, bf16[128,16]{1,0:T(8,128)(2,1)S(1)}, u32[]{:S(2)}, u32[]{:S(2)}) collective-permute-start(bf16[128,16]{1,0:T(8,128)(2,1)S(1)} %copy-done.11), channel_id=1, source_target_pairs={{8,20},{10,22},{16,12},{18,14},{24,4},{26,6},{28,0},{30,2},{20,8},... | collective-permute-start | bytes 12296 | tf_op jit(solution)/shard_map/ppermute | solution.py:124
  66.9 42.0 %collective-permute-start.18 = (bf16[128,16]{1,0:T(8,128)(2,1)S(1)}, bf16[128,16]{1,0:T(8,128)(2,1)S(1)}, u32[]{:S(2)}, u32[]{:S(2)}) collective-permute-start(bf16[128,16]{1,0:T(8,128)(2,1)S(1)} %copy-done.11), channel_id=1, source_target_pairs={{8,24},{10,26},{16,28},{18,30},{24,20},{26,22},{28,12},{30,14},{20... | collective-permute-start | bytes 12296 | tf_op jit(solution)/shard_map/ppermute | solution.py:124
  69.3 5.3 %copy-start.10 = (bf16[64,2048]{1,0:T(8,128)(2,1)S(1)}, bf16[64,2048]{1,0:T(8,128)(2,1)}, u32[]{:S(2)}) copy-start(bf16[64,2048]{1,0:T(8,128)(2,1)} %shard_map.67) | copy-start | bytes 786436
  69.3 39.5 %collective-permute-start.19 = (bf16[128,16]{1,0:T(8,128)(2,1)S(1)}, bf16[128,16]{1,0:T(8,128)(2,1)S(1)}, u32[]{:S(2)}, u32[]{:S(2)}) collective-permute-start(bf16[128,16]{1,0:T(8,128)(2,1)S(1)} %copy-done.11), channel_id=1, source_target_pairs={{8,4},{10,6},{16,0},{18,2},{24,8},{26,10},{28,16},{30,18},{20,24},... | collective-permute-start | bytes 12296 | tf_op jit(solution)/shard_map/ppermute | solution.py:124
  74.6 6.8 %copy-start.2 = (f32[256,2048]{1,0:T(8,128)S(1)}, f32[256,2048]{1,0:T(8,128)}, u32[]{:S(2)}) copy-start(f32[256,2048]{1,0:T(8,128)} %copy-done.1) | copy-start | bytes 6291460
  74.6 6.4 %collective-permute-start.9 = (bf16[64,2048]{1,0:T(8,128)(2,1)S(1)}, bf16[64,2048]{1,0:T(8,128)(2,1)S(1)}, u32[]{:S(2)}, u32[]{:S(2)}) collective-permute-start(bf16[64,2048]{1,0:T(8,128)(2,1)S(1)} %copy-done.10), channel_id=1, source_target_pairs={{8,16},{10,18},{16,24},{18,26},{24,28},{26,30},{28,20},{30,22},{20... | collective-permute-start | bytes 786440 | tf_op jit(solution)/shard_map/ppermute | solution.py:124
  74.7 6.6 %collective-permute-start.12 = (bf16[64,2048]{1,0:T(8,128)(2,1)}, bf16[64,2048]{1,0:T(8,128)(2,1)S(1)}, u32[]{:S(2)}, u32[]{:S(2)}) collective-permute-start(bf16[64,2048]{1,0:T(8,128)(2,1)} %shard_map.69), channel_id=1, source_target_pairs={{8,0},{10,2},{16,8},{18,10},{24,16},{26,18},{28,24},{30,26},{20,28... | collective-permute-start | bytes 786440 | tf_op jit(solution)/shard_map/ppermute | solution.py:124
  91.6 15.0 %collective-permute-start.14 = (bf16[64,2048]{1,0:T(8,128)(2,1)S(1)}, bf16[64,2048]{1,0:T(8,128)(2,1)S(1)}, u32[]{:S(2)}, u32[]{:S(2)}) collective-permute-start(bf16[64,2048]{1,0:T(8,128)(2,1)S(1)} %get-tuple-element.11), channel_id=1, source_target_pairs={{8,16},{10,18},{16,24},{18,26},{24,28},{26,30},{28,20},{30,22},{20... | collective-permute-start | bytes 786440 | tf_op jit(solution)/shard_map/ppermute | solution.py:124
  92.1 14.4 %collective-permute-start.22 = (bf16[64,2048]{1,0:T(8,128)(2,1)S(1)}, bf16[64,2048]{1,0:T(8,128)(2,1)S(1)}, u32[]{:S(2)}, u32[]{:S(2)}) collective-permute-start(bf16[64,2048]{1,0:T(8,128)(2,1)S(1)} %get-tuple-element.12), channel_id=1, source_target_pairs={{8,0},{10,2},{16,8},{18,10},{24,16},{26,18},{28,24},{30,26},{20,28... | collective-permute-start | bytes 786440 | tf_op jit(solution)/shard_map/ppermute | solution.py:124
  106.7 14.8 %collective-permute-start.17 = (bf16[128,2048]{1,0:T(8,128)(2,1)S(1)}, bf16[128,2048]{1,0:T(8,128)(2,1)S(1)}, u32[]{:S(2)}, u32[]{:S(2)}) collective-permute-start(bf16[128,2048]{1,0:T(8,128)(2,1)S(1)} %get-tuple-element.9), channel_id=1, source_target_pairs={{8,16},{10,18},{16,24},{18,26},{24,28},{26,30},{28,20},{30,22},{20... | collective-permute-start | bytes 1572872 | tf_op jit(solution)/shard_map/ppermute | solution.py:124
  107.1 14.5 %collective-permute-start.23 = (bf16[128,2048]{1,0:T(8,128)(2,1)S(1)}, bf16[128,2048]{1,0:T(8,128)(2,1)S(1)}, u32[]{:S(2)}, u32[]{:S(2)}) collective-permute-start(bf16[128,2048]{1,0:T(8,128)(2,1)S(1)} %get-tuple-element.10), channel_id=1, source_target_pairs={{8,0},{10,2},{16,8},{18,10},{24,16},{26,18},{28,24},{30,26},{20,28... | collective-permute-start | bytes 1572872 | tf_op jit(solution)/shard_map/ppermute | solution.py:124
  121.9 13.2 %collective-permute-start.20 = (bf16[128,2048]{1,0:T(8,128)(2,1)S(1)}, bf16[128,2048]{1,0:T(8,128)(2,1)S(1)}, u32[]{:S(2)}, u32[]{:S(2)}) collective-permute-start(bf16[128,2048]{1,0:T(8,128)(2,1)S(1)} %get-tuple-element.7), channel_id=1, source_target_pairs={{8,16},{10,18},{16,24},{18,26},{24,28},{26,30},{28,20},{30,22},{20... | collective-permute-start | bytes 1572872 | tf_op jit(solution)/shard_map/ppermute | solution.py:124
  122.3 15.7 %copy-start = (bf16[1,2,2048,384]{3,2,1,0:T(8,128)(2,1)S(1)}, bf16[1,2,2048,384]{3,2,1,0:T(8,128)(2,1)}, u32[]{:S(2)}) copy-start(bf16[1,2,2048,384]{3,2,1,0:T(8,128)(2,1)} %param.9) | copy-start | bytes 9437188
  122.3 15.7 %copy-start.5 = (bf16[128,16]{1,0:T(8,128)(2,1)S(1)}, bf16[128,16]{1,0:T(8,128)(2,1)}, u32[]{:S(2)}) copy-start(bf16[128,16]{1,0:T(8,128)(2,1)} %copy.20.value_ref.gate_ref) | copy-start | bytes 12292
  122.3 15.7 %copy-start.6 = (bf16[128,2048]{1,0:T(8,128)(2,1)S(1)}, bf16[128,2048]{1,0:T(8,128)(2,1)}, u32[]{:S(2)}) copy-start(bf16[128,2048]{1,0:T(8,128)(2,1)} %x_ref.1) | copy-start | bytes 1572868
  122.3 13.2 %collective-permute-start.24 = (bf16[128,2048]{1,0:T(8,128)(2,1)S(1)}, bf16[128,2048]{1,0:T(8,128)(2,1)S(1)}, u32[]{:S(2)}, u32[]{:S(2)}) collective-permute-start(bf16[128,2048]{1,0:T(8,128)(2,1)S(1)} %get-tuple-element.8), channel_id=1, source_target_pairs={{8,0},{10,2},{16,8},{18,10},{24,16},{26,18},{28,24},{30,26},{20,28... | collective-permute-start | bytes 1572872 | tf_op jit(solution)/shard_map/ppermute | solution.py:124
  135.8 11.8 %collective-permute-start.21 = (bf16[128,2048]{1,0:T(8,128)(2,1)S(1)}, bf16[128,2048]{1,0:T(8,128)(2,1)S(1)}, u32[]{:S(2)}, u32[]{:S(2)}) collective-permute-start(bf16[128,2048]{1,0:T(8,128)(2,1)S(1)} %get-tuple-element.5), channel_id=1, source_target_pairs={{8,16},{10,18},{16,24},{18,26},{24,28},{26,30},{28,20},{30,22},{20... | collective-permute-start | bytes 1572872 | tf_op jit(solution)/shard_map/ppermute | solution.py:124
  137.1 10.5 %collective-permute-start.25 = (bf16[128,2048]{1,0:T(8,128)(2,1)S(1)}, bf16[128,2048]{1,0:T(8,128)(2,1)S(1)}, u32[]{:S(2)}, u32[]{:S(2)}) collective-permute-start(bf16[128,2048]{1,0:T(8,128)(2,1)S(1)} %get-tuple-element.6), channel_id=1, source_target_pairs={{8,0},{10,2},{16,8},{18,10},{24,16},{26,18},{28,24},{30,26},{20,28... | collective-permute-start | bytes 1572872 | tf_op jit(solution)/shard_map/ppermute | solution.py:124
  (6 other events, 12.4 us)

commit v3 on v1

--- a/solution.py
+++ b/solution.py
@@ -19,10 +19,58 @@
     return walk + list(range(rows_n - 1, -1, -1))
 
 
-def ffn_kernel(x_ref, gate_ref, g0, u0, d0, g1, u1, d1, out_ref):
+def gates_kernel(chips_n, gate_ref, out_ref, send_sems, recv_sems):
+    me = lax.axis_index("expert")
+    chip, core = me // 2, me % 2
+    peers = [{"expert": (chip + d) % chips_n * 2 + core} for d in range(1, chips_n)]
+    barrier = pltpu.get_barrier_semaphore()
+    for peer in peers:
+        pl.semaphore_signal(barrier, inc=1, device_id=peer, device_id_type=pl.DeviceIdType.MESH)
+    pl.semaphore_wait(barrier, chips_n - 1)
+    copies = []
+    for i, peer in enumerate(peers):
+        copies.append(
+            pltpu.make_async_remote_copy(
+                src_ref=gate_ref,
+                dst_ref=out_ref.at[i + 1],
+                send_sem=send_sems.at[i],
+                recv_sem=recv_sems.at[i],
+                device_id=peer,
+                device_id_type=pl.DeviceIdType.MESH,
+            )
+        )
+        copies[i].start()
+    out_ref[0] = gate_ref[...]
+    for copy in copies:
+        copy.wait()
+
+
+def share_gates(dense, chips_n):
+    return pl.pallas_call(
+        functools.partial(gates_kernel, chips_n),
+        out_shape=jax.ShapeDtypeStruct((chips_n,) + dense.shape, dense.dtype),
+        in_specs=[pl.BlockSpec(memory_space=pltpu.VMEM)],
+        out_specs=pl.BlockSpec(memory_space=pltpu.VMEM),
+        scratch_shapes=[pltpu.SemaphoreType.DMA((chips_n - 1,))] * 2,
+        compiler_params=pltpu.CompilerParams(collective_id=0, has_side_effects=True),
+    )(dense)
+
+
+def ffn_kernel(cycle, distances, x_ref, gate_ref, g0, u0, d0, g1, u1, d1, earlier_ref, out_ref):
     i = pl.program_id(0)
     x = x_ref[...]
-    weight = jnp.where(i % 2 == 0, gate_ref[:, 0:1], gate_ref[:, 1:2])
+    chips_n = len(cycle)
+    chip = lax.axis_index("expert") // 2
+    place = sum(jnp.where(chip == c, p, 0) for p, c in enumerate(cycle))
+    lanes = lax.broadcasted_iota(jnp.int32, gate_ref.shape[1:], 1)
+    weights = []
+    for distance in distances:
+        there = (place + distance + chips_n) % chips_n
+        source = sum(jnp.where(there == p, c, 0) for p, c in enumerate(cycle))
+        gates = gate_ref[(chip - source + chips_n) % chips_n].astype(jnp.float32)
+        picked = jnp.where(lanes == chip * 2 + i % 2, gates, 0.0)
+        weights.append(jnp.sum(picked, axis=1, keepdims=True))
+    weight = jnp.concatenate(weights)
 
     def add(g_ref, u_ref, d_ref, first):
         gate_h = jnp.dot(x, g_ref[0], preferred_element_type=jnp.float32)
@@ -53,7 +101,7 @@
         add(g1, u1, d1, False)
 
 
-def ffn(x, gates, own, other):
+def ffn(cycle, distances, x, gates, own, other, earlier):
     rows, width = x.shape
     half = own[0].shape[2]
 
@@ -66,39 +114,34 @@
     flops = 4 * 2 * 3 * rows * width * half
     moved = 4 * 3 * width * half * 2 + rows * width * 6
     return pl.pallas_call(
-        ffn_kernel,
+        functools.partial(ffn_kernel, cycle, distances),
         grid=(4,),
         out_shape=jax.ShapeDtypeStruct((rows, width), jnp.float32),
         in_specs=[
             pl.BlockSpec((rows, width), lambda i: (0, 0)),
-            pl.BlockSpec((rows, 2), lambda i: (0, 0)),
+            pl.BlockSpec(gates.shape, lambda i: (0, 0, 0)),
             early((width, half)),
             early((width, half)),
             early((half, width)),
             late((width, half)),
             late((width, half)),
             late((half, width)),
+            pl.BlockSpec(memory_space=pl.ANY),
         ],
         out_specs=pl.BlockSpec((rows, width), lambda i: (0, 0)),
         cost_estimate=pl.CostEstimate(
             flops=flops, bytes_accessed=moved, transcendentals=4 * rows * half
         ),
         compiler_params=pltpu.CompilerParams(vmem_limit_bytes=48 * 2**20),
-    )(x, gates, *own, *other)
+    )(x, gates, *own, *other, earlier)
 
 
 def on_device(cycle, tokens, expert_ids, route_weight, w_gate, w_up, w_down):
     devices_n = lax.axis_size("expert")
-    index = lax.axis_index("expert")
     chips_n = devices_n // 2
-    chip, core = index // 2, index % 2
     rows = tokens.shape[0]
     cut = rows // 2
     far = chips_n // 2
-    place = [0] * chips_n
-    for i, c in enumerate(cycle):
-        place[c] = i
-
     def turn(step):
         pairs = []
         for i, c in enumerate(cycle):
@@ -111,23 +154,12 @@
     send = lambda value, pairs: lax.ppermute(value, "expert", pairs)
 
     gates = (route_weight / jnp.sum(route_weight, axis=1, keepdims=True)).astype(jnp.bfloat16)
-    chosen = expert_ids[:, :, None] == jnp.arange(devices_n, dtype=jnp.int32)
+    lanes = -(-devices_n // 128) * 128
+    chosen = expert_ids[:, :, None] == jnp.arange(lanes, dtype=jnp.int32)
     dense = jnp.sum(jnp.where(chosen, gates.astype(jnp.float32)[:, :, None], 0.0), axis=1)
 
     own = (w_gate[0], w_up[0], w_down[0])
     other = tuple(send(w, swap) for w in own)
-    all_gates = lax.all_gather(dense.astype(jnp.bfloat16), "expert")
-    all_gates = all_gates.reshape(chips_n, 2, rows, devices_n)
-    all_gates = lax.dynamic_index_in_dim(all_gates, core, 1, keepdims=False)
-    all_gates = lax.dynamic_slice_in_dim(all_gates, 2 * chip, 2, 2).astype(jnp.float32)
-    here = jnp.array(place, jnp.int32)[chip]
-    walk = jnp.array(cycle, jnp.int32)
-
-    def gates_at(distance):
-        return lax.dynamic_index_in_dim(
-            all_gates, walk[(here + distance + chips_n) % chips_n], 0, keepdims=False
-        )
-
     from_left, from_right = {0: tokens}, {0: tokens}
     for s in range(1, far):
         from_left[s] = send(from_left[s - 1], right)
@@ -135,25 +167,25 @@
     far_block = jnp.concatenate(
         [send(from_left[far - 1][:cut], right), send(from_right[far - 1][cut:], left)]
     )
-
-    def outputs(blocks, distances):
+    all_gates = share_gates(dense.astype(jnp.bfloat16), chips_n)
+
+    def outputs(blocks, distances, earlier):
         x = jnp.concatenate(blocks) if len(blocks) > 1 else blocks[0]
-        g = jnp.concatenate([gates_at(d) for d in distances])
-        return ffn(x, g, own, other)
-
-    near = outputs([from_left[1], from_right[1], tokens], [-1, 1, 0])
-    for_left, for_right = {1: near[:rows]}, {1: near[rows : 2 * rows]}
-    mine = near[2 * rows :]
-    for s in range(2, far):
-        both = outputs([from_left[s], from_right[s]], [-s, s])
+        return ffn(cycle, distances, x, all_gates, own, other, earlier)
+
+    last = outputs([far_block], [far], far_block)
+    for_left, for_right = {}, {}
+    for s in range(1, far):
+        both = outputs([from_left[s], from_right[s]], [-s, s], last)
         for_left[s], for_right[s] = both[:rows], both[rows:]
-    last = outputs([far_block], [far])
 
     to_right = send(last[:cut].astype(jnp.bfloat16), right)
     to_left = send(last[cut:].astype(jnp.bfloat16), left)
     to_right = jnp.pad(to_right, ((0, cut), (0, 0)))
     to_left = jnp.pad(to_left, ((cut, 0), (0, 0)))
     for s in range(far - 1, 0, -1):
+        if s == 1:
+            mine = outputs([tokens], [0], to_right)
         to_right = send((to_right.astype(jnp.float32) + for_right[s]).astype(jnp.bfloat16), right)
         to_left = send((to_left.astype(jnp.float32) + for_left[s]).astype(jnp.bfloat16), left)
     total = mine + to_right.astype(jnp.float32) + to_left.astype(jnp.float32)

time: 160 us -> 133 us (0.83)
  blocking collectives: 22 us -> 0 us
  between operations: 20.8 us -> 0.31 us
  Pallas kernels: 50.8 us -> 69.2 us
  waiting for transfers between devices: 38 us -> 33.2 us
  other arithmetic: 5.57 us -> 7.81 us
    all_gather x1 -> x0, blocking collectives: 22 us -> none  [on_device(): all_gates = lax.all_gather(dense.astype(jnp.bfloat16), 'expert')]
    pallas_call x4 -> x6, Pallas kernels: 50.8 us -> 69.2 us  [the longest x5 57.3 us: ffn(): pl.pallas_call(functools.partial(ffn_kernel, cycle, distances), grid=(4,)...]
    ppermute x19, waiting for transfers between devices: 38 us -> 33.2 us  [on_device(): send = lambda value, pairs: lax.ppermute(value, 'expert', pairs)]
    dynamic_slice x9 -> x0, local copies, waits for them, and re-layouts: 3.47 us -> none  [the longest x1 1.65 us: gates_at(): walk[(here + distance + chips_n) % chips_n]]
    slice x1, local copies, waits for them, and re-layouts: 0.02 us -> 1.66 us  [on_device(): from_left[far - 1][:cut]]
    unnamed x8 -> x23, local copies, waits for them, and re-layouts: 0.02 us -> 1.63 us
  transfers between devices with their start and end apart: 19 -> 19, of which waited for: 6 -> 3; matrix products, arithmetic and copies ran while one was open for 5% -> 7% of each run, Pallas kernels for 26% -> 45%
where the time goes in v3:
time: 133 us
  Pallas kernels  69.2 us (52%)
  waiting for transfers between devices  33.2 us (25%)
  starting transfers between devices  18.2 us (14%)
  other arithmetic  7.81 us (6%)
  local copies, waits for them, and re-layouts  4.16 us (3%)
    pallas_call x5, Pallas kernels, ffn(): pl.pallas_call(functools.partial(ffn_kernel, cycle, distances), grid=(4,)...  57.3 us
    ppermute x19, waiting for transfers between devices, on_device(): send = lambda value, pairs: lax.ppermute(value, 'expert', pairs)  33.2 us
    ppermute x19, starting transfers between devices, on_device(): send = lambda value, pairs: lax.ppermute(value, 'expert', pairs)  18.2 us
    pallas_call x1, Pallas kernels, share_gates(): pl.pallas_call(functools.partial(gates_kernel, chips_n), out_shape=jax.Sh...  11.8 us
  transfers between devices with their start and end apart: 19, of which 3 were waited for; matrix products, arithmetic and copies ran while one was open for 7% of the time, Pallas kernels for 45%

profile of v3, /device:TPU:0, one launch (start us, length us, event | category | flops | bytes accessed | tf_op | source)
XLA Modules:
  0.0 132.9 jit_solution(13774692310969267978)
XLA Ops:
  1.0 2.5 %collective-permute-start.7 = (bf16[128,2048]{1,0:T(8,128)(2,1)}, bf16[128,2048]{1,0:T(8,128)(2,1)S(1)}, u32[]{:S(2)}, u32[]{:S(2)}) collective-permute-start(bf16[128,2048]{1,0:T(8,128)(2,1)} %x_ref.1), channel_id=1, source_target_pairs={{8,0},{10,2},{16,8},{18,10},{24,16},{26,18},{28,24},{30,26},{20,28... | collective-permute-start | bytes 1572872 | tf_op jit(solution)/shard_map/ppermute | solution.py:154
  3.5 12.8 %collective-permute-done.7 = bf16[128,2048]{1,0:T(8,128)(2,1)S(1)} collective-permute-done((bf16[128,2048]{1,0:T(8,128)(2,1)}, bf16[128,2048]{1,0:T(8,128)(2,1)S(1)}, u32[]{:S(2)}, u32[]{:S(2)}) %collective-permute-start.7) | collective-permute-done | bytes 524320 | tf_op jit(solution)/shard_map/ppermute | solution.py:154
  16.3 1.7 %collective-permute-start.8 = (bf16[128,2048]{1,0:T(8,128)(2,1)S(1)}, bf16[128,2048]{1,0:T(8,128)(2,1)S(1)}, u32[]{:S(2)}, u32[]{:S(2)}) collective-permute-start(bf16[128,2048]{1,0:T(8,128)(2,1)S(1)} %collective-permute-done.7), channel_id=1, source_target_pairs={{8,0},{10,2},{16,8},{18,10},{24,16},{26,18},{28,24},{30,26},{20,28... | collective-permute-start | bytes 1572872 | tf_op jit(solution)/shard_map/ppermute | solution.py:154
  18.4 11.7 %collective-permute-done.8 = bf16[128,2048]{1,0:T(8,128)(2,1)S(1)} collective-permute-done((bf16[128,2048]{1,0:T(8,128)(2,1)S(1)}, bf16[128,2048]{1,0:T(8,128)(2,1)S(1)}, u32[]{:S(2)}, u32[]{:S(2)}) %collective-permute-start.8) | collective-permute-done | bytes 524320 | tf_op jit(solution)/shard_map/ppermute | solution.py:154
  30.1 1.5 %collective-permute-start.9 = (bf16[128,2048]{1,0:T(8,128)(2,1)S(1)}, bf16[128,2048]{1,0:T(8,128)(2,1)S(1)}, u32[]{:S(2)}, u32[]{:S(2)}) collective-permute-start(bf16[128,2048]{1,0:T(8,128)(2,1)S(1)} %collective-permute-done.8), channel_id=1, source_target_pairs={{8,0},{10,2},{16,8},{18,10},{24,16},{26,18},{28,24},{30,26},{20,28... | collective-permute-start | bytes 1572872 | tf_op jit(solution)/shard_map/ppermute | solution.py:154
  32.1 0.7 reduce_sum.18
  33.6 0.8 copy.9
  34.4 8.7 %collective-permute-done.9 = bf16[128,2048]{1,0:T(8,128)(2,1)S(1)} collective-permute-done((bf16[128,2048]{1,0:T(8,128)(2,1)S(1)}, bf16[128,2048]{1,0:T(8,128)(2,1)S(1)}, u32[]{:S(2)}, u32[]{:S(2)}) %collective-permute-start.9) | collective-permute-done | bytes 524320 | tf_op jit(solution)/shard_map/ppermute | solution.py:154
  43.1 0.8 copy-done.4
  43.9 0.7 slice.43
  44.6 1.3 collective-permute-start.10
  45.9 1.7 %slice.42 = bf16[64,2048]{1,0:T(8,128)(2,1)} slice(bf16[128,2048]{1,0:T(8,128)(2,1)} %collective-permute-done.5), slice={[0:64], [0:2048]} | slice | bytes 524288 | tf_op jit(solution)/shard_map/slice | solution.py:168
  47.6 1.0 collective-permute-start.6
  48.5 1.0 select_reduce_fusion.gate_ref
  49.5 11.8 %shard_map.64.gate_ref = bf16[8,128,128]{2,1,0:T(8,128)(2,1)} custom-call(bf16[128,128]{1,0:T(8,128)(2,1)} %select_reduce_fusion.gate_ref), custom_call_target="tpu_custom_call" | custom-call | tf_op jit(solution)/shard_map/pallas_call | solution.py:49
  61.4 1.3 %pad_maximum_fusion.x_ref = bf16[256,2048]{1,0:T(8,128)(2,1)S(1)} fusion(bf16[128,2048]{1,0:T(8,128)(2,1)} %copy-done.4, bf16[128,2048]{1,0:T(8,128)(2,1)} %collective-permute-done.5), kind=kLoop, calls=%fused_computation.12 | loop fusion | flops 2097152 | bytes 2097152 | tf_op jit(solution)/shard_map/concatenate | solution.py:173
  62.8 1.1 pad_maximum_fusion.3.x_ref.earlier_ref
  63.9 9.6 %shard_map.65.earlier_ref = f32[128,2048]{1,0:T(8,128)S(1)} custom-call(bf16[128,2048]{1,0:T(8,128)(2,1)S(1)} %pad_maximum_fusion.3.x_ref.earlier_ref, bf16[8,128,128]{2,1,0:T(8,128)(2,1)S(1)} %copy-done.2, bf16[2,2048,384]{2,1,0:T(8,128)(2,1)S(1)} %bitcast.7, bf16[2,2048,384]{2,1,0:T(8,128)(2,1)} %bitcast.10, bf16[2,384,2048]{2,1,0:T(8,128)(2,1)} %bitcast.16, ...), custom_call_target="tpu_custom_call" | custom-call | flops 2415919104 | bytes 20447232 | tf_op jit(solution)/shard_map/pallas_call | solution.py:116
  73.6 1.3 collective-permute-start.11
  74.9 0.8 collective-permute-start.15
  75.7 12.7 %shard_map.66 = f32[256,2048]{1,0:T(8,128)S(1)} custom-call(bf16[256,2048]{1,0:T(8,128)(2,1)S(1)} %pad_maximum_fusion.x_ref, bf16[8,128,128]{2,1,0:T(8,128)(2,1)S(1)} %copy-done.2, bf16[2,2048,384]{2,1,0:T(8,128)(2,1)} %bitcast.4, bf16[2,2048,384]{2,1,0:T(8,128)(2,1)} %bitcast.11, bf16[2,384,2048]{2,1,0:T(8,128)(2,1)} %bitcast.17, ...), custom_call_target="tpu_custom_call" | custom-call | flops 4831838208 | bytes 22020096 | tf_op jit(solution)/shard_map/pallas_call | solution.py:116
  88.6 1.3 collective-permute-start.12
  89.9 0.8 collective-permute-start.16
  90.7 1.1 pad_maximum_fusion.1.x_ref
  91.9 12.7 %shard_map.67 = f32[256,2048]{1,0:T(8,128)S(1)} custom-call(bf16[256,2048]{1,0:T(8,128)(2,1)S(1)} %pad_maximum_fusion.1.x_ref, bf16[8,128,128]{2,1,0:T(8,128)(2,1)S(1)} %copy-done.2, bf16[2,2048,384]{2,1,0:T(8,128)(2,1)} %bitcast.5, bf16[2,2048,384]{2,1,0:T(8,128)(2,1)} %bitcast.12, bf16[2,384,2048]{2,1,0:T(8,128)(2,1)} %bitcast.18, ...), custom_call_target="tpu_custom_call" | custom-call | flops 4831838208 | bytes 22020096 | tf_op jit(solution)/shard_map/pallas_call | solution.py:116
  104.9 1.3 collective-permute-start.13
  106.2 0.8 collective-permute-start.17
  107.1 12.7 %shard_map.69 = f32[256,2048]{1,0:T(8,128)S(1)} custom-call(bf16[256,2048]{1,0:T(8,128)(2,1)S(1)} %pad_maximum_fusion.2.x_ref, bf16[8,128,128]{2,1,0:T(8,128)(2,1)S(1)} %copy-done.2, bf16[2,2048,384]{2,1,0:T(8,128)(2,1)} %bitcast.6, bf16[2,2048,384]{2,1,0:T(8,128)(2,1)} %bitcast.13, bf16[2,384,2048]{2,1,0:T(8,128)(2,1)} %bitcast.19, ...), custom_call_target="tpu_custom_call" | custom-call | flops 4831838208 | bytes 22020096 | tf_op jit(solution)/shard_map/pallas_call | solution.py:116
  120.2 1.3 collective-permute-start.14
  121.5 0.8 collective-permute-start.18
  122.2 9.6 %shard_map.68 = f32[128,2048]{1,0:T(8,128)S(1)} custom-call(bf16[128,2048]{1,0:T(8,128)(2,1)S(1)} %copy-done.3, bf16[8,128,128]{2,1,0:T(8,128)(2,1)S(1)} %copy-done.2, bf16[2,2048,384]{2,1,0:T(8,128)(2,1)S(1)} %bitcast.8, bf16[2,2048,384]{2,1,0:T(8,128)(2,1)} %bitcast.14, bf16[2,384,2048]{2,1,0:T(8,128)(2,1)} %bitcast.20, ...), custom_call_target="tpu_custom_call" | custom-call | flops 2415919104 | bytes 20447232 | tf_op jit(solution)/shard_map/pallas_call | solution.py:116
  131.9 1.0 add_convert_fusion
  (51 shorter events, 3.7 us)
Async XLA Ops:
  0.0 63.8 %collective-permute-start = (bf16[2,2048,384]{2,1,0:T(8,128)(2,1)}, bf16[2,2048,384]{2,1,0:T(8,128)(2,1)}, u32[]{:S(2)}, u32[]{:S(2)}) collective-permute-start(bf16[2,2048,384]{2,1,0:T(8,128)(2,1)} %bitcast.3), channel_id=1, source_target_pairs={{0,2},{2,0},{4,6},{6,4},{8,10},{10,8},{12,14},{14,12},{16,18},{18,... | collective-permute-start | bytes 9437192 | tf_op jit(solution)/shard_map/ppermute | solution.py:154
  0.5 63.4 %collective-permute-start.1 = (bf16[2,2048,384]{2,1,0:T(8,128)(2,1)}, bf16[2,2048,384]{2,1,0:T(8,128)(2,1)}, u32[]{:S(2)}, u32[]{:S(2)}) collective-permute-start(bf16[2,2048,384]{2,1,0:T(8,128)(2,1)} %bitcast.9), channel_id=1, source_target_pairs={{0,2},{2,0},{4,6},{6,4},{8,10},{10,8},{12,14},{14,12},{16,18},{18,... | collective-permute-start | bytes 9437192 | tf_op jit(solution)/shard_map/ppermute | solution.py:154
  0.5 63.4 %collective-permute-start.2 = (bf16[2,384,2048]{2,1,0:T(8,128)(2,1)}, bf16[2,384,2048]{2,1,0:T(8,128)(2,1)}, u32[]{:S(2)}, u32[]{:S(2)}) collective-permute-start(bf16[2,384,2048]{2,1,0:T(8,128)(2,1)} %bitcast.15), channel_id=1, source_target_pairs={{0,2},{2,0},{4,6},{6,4},{8,10},{10,8},{12,14},{14,12},{16,18},{18,... | collective-permute-start | bytes 9437192 | tf_op jit(solution)/shard_map/ppermute | solution.py:154
  1.0 15.4 %collective-permute-start.7 = (bf16[128,2048]{1,0:T(8,128)(2,1)}, bf16[128,2048]{1,0:T(8,128)(2,1)S(1)}, u32[]{:S(2)}, u32[]{:S(2)}) collective-permute-start(bf16[128,2048]{1,0:T(8,128)(2,1)} %x_ref.1), channel_id=1, source_target_pairs={{8,0},{10,2},{16,8},{18,10},{24,16},{26,18},{28,24},{30,26},{20,28... | collective-permute-start | bytes 1572872 | tf_op jit(solution)/shard_map/ppermute | solution.py:154
  3.5 14.6 %collective-permute-start.3 = (bf16[128,2048]{1,0:T(8,128)(2,1)}, bf16[128,2048]{1,0:T(8,128)(2,1)S(1)}, u32[]{:S(2)}, u32[]{:S(2)}) collective-permute-start(bf16[128,2048]{1,0:T(8,128)(2,1)} %x_ref.1), channel_id=1, source_target_pairs={{8,16},{10,18},{16,24},{18,26},{24,28},{26,30},{28,20},{30,22},{20... | collective-permute-start | bytes 1572872 | tf_op jit(solution)/shard_map/ppermute | solution.py:154
  16.3 2.0 %copy-start.5 = (bf16[128,2048]{1,0:T(8,128)(2,1)}, bf16[128,2048]{1,0:T(8,128)(2,1)S(1)}, u32[]{:S(2)}) copy-start(bf16[128,2048]{1,0:T(8,128)(2,1)S(1)} %collective-permute-done.7) | copy-start | bytes 1572868
  16.3 13.8 %collective-permute-start.8 = (bf16[128,2048]{1,0:T(8,128)(2,1)S(1)}, bf16[128,2048]{1,0:T(8,128)(2,1)S(1)}, u32[]{:S(2)}, u32[]{:S(2)}) collective-permute-start(bf16[128,2048]{1,0:T(8,128)(2,1)S(1)} %collective-permute-done.7), channel_id=1, source_target_pairs={{8,0},{10,2},{16,8},{18,10},{24,16},{26,18},{28,24},{30,26},{20,28... | collective-permute-start | bytes 1572872 | tf_op jit(solution)/shard_map/ppermute | solution.py:154
  18.0 12.1 %copy-start.7 = (bf16[128,2048]{1,0:T(8,128)(2,1)}, bf16[128,2048]{1,0:T(8,128)(2,1)S(1)}, u32[]{:S(2)}) copy-start(bf16[128,2048]{1,0:T(8,128)(2,1)S(1)} %collective-permute-done.3) | copy-start | bytes 1572868
  18.0 13.6 %collective-permute-start.4 = (bf16[128,2048]{1,0:T(8,128)(2,1)S(1)}, bf16[128,2048]{1,0:T(8,128)(2,1)}, u32[]{:S(2)}, u32[]{:S(2)}) collective-permute-start(bf16[128,2048]{1,0:T(8,128)(2,1)S(1)} %collective-permute-done.3), channel_id=1, source_target_pairs={{8,16},{10,18},{16,24},{18,26},{24,28},{26,30},{28,20},{30,22},{20... | collective-permute-start | bytes 1572872 | tf_op jit(solution)/shard_map/ppermute | solution.py:154
  30.1 13.0 %copy-start.9 = (bf16[128,2048]{1,0:T(8,128)(2,1)}, bf16[128,2048]{1,0:T(8,128)(2,1)S(1)}, u32[]{:S(2)}) copy-start(bf16[128,2048]{1,0:T(8,128)(2,1)S(1)} %collective-permute-done.8) | copy-start | bytes 1572868
  30.1 13.0 %collective-permute-start.9 = (bf16[128,2048]{1,0:T(8,128)(2,1)S(1)}, bf16[128,2048]{1,0:T(8,128)(2,1)S(1)}, u32[]{:S(2)}, u32[]{:S(2)}) collective-permute-start(bf16[128,2048]{1,0:T(8,128)(2,1)S(1)} %collective-permute-done.8), channel_id=1, source_target_pairs={{8,0},{10,2},{16,8},{18,10},{24,16},{26,18},{28,24},{30,26},{20,28... | collective-permute-start | bytes 1572872 | tf_op jit(solution)/shard_map/ppermute | solution.py:154
  31.6 14.3 %collective-permute-start.5 = (bf16[128,2048]{1,0:T(8,128)(2,1)}, bf16[128,2048]{1,0:T(8,128)(2,1)}, u32[]{:S(2)}, u32[]{:S(2)}) collective-permute-start(bf16[128,2048]{1,0:T(8,128)(2,1)} %collective-permute-done.4), channel_id=1, source_target_pairs={{8,16},{10,18},{16,24},{18,26},{24,28},{26,30},{28,20},{30,22},{20... | collective-permute-start | bytes 1572872 | tf_op jit(solution)/shard_map/ppermute | solution.py:154
  43.1 0.8 copy-start.4
  44.6 19.2 %copy-start = (bf16[1,2,2048,384]{3,2,1,0:T(8,128)(2,1)S(1)}, bf16[1,2,2048,384]{3,2,1,0:T(8,128)(2,1)}, u32[]{:S(2)}) copy-start(bf16[1,2,2048,384]{3,2,1,0:T(8,128)(2,1)} %param.9) | copy-start | bytes 9437188
  44.6 18.1 %collective-permute-start.10 = (bf16[64,2048]{1,0:T(8,128)(2,1)}, bf16[64,2048]{1,0:T(8,128)(2,1)}, u32[]{:S(2)}, u32[]{:S(2)}) collective-permute-start(bf16[64,2048]{1,0:T(8,128)(2,1)} %slice.43), channel_id=1, source_target_pairs={{8,0},{10,2},{16,8},{18,10},{24,16},{26,18},{28,24},{30,26},{20,28... | collective-permute-start | bytes 786440 | tf_op jit(solution)/shard_map/ppermute | solution.py:154
  47.6 15.2 %collective-permute-start.6 = (bf16[64,2048]{1,0:T(8,128)(2,1)}, bf16[64,2048]{1,0:T(8,128)(2,1)}, u32[]{:S(2)}, u32[]{:S(2)}) collective-permute-start(bf16[64,2048]{1,0:T(8,128)(2,1)} %slice.42), channel_id=1, source_target_pairs={{8,16},{10,18},{16,24},{18,26},{24,28},{26,30},{28,20},{30,22},{20... | collective-permute-start | bytes 786440 | tf_op jit(solution)/shard_map/ppermute | solution.py:154
  61.4 2.5 %copy-start.2 = (bf16[8,128,128]{2,1,0:T(8,128)(2,1)S(1)}, bf16[8,128,128]{2,1,0:T(8,128)(2,1)}, u32[]{:S(2)}) copy-start(bf16[8,128,128]{2,1,0:T(8,128)(2,1)} %shard_map.64.gate_ref) | copy-start | bytes 786436
  73.6 14.8 %collective-permute-start.11 = (bf16[64,2048]{1,0:T(8,128)(2,1)S(1)}, bf16[64,2048]{1,0:T(8,128)(2,1)S(1)}, u32[]{:S(2)}, u32[]{:S(2)}) collective-permute-start(bf16[64,2048]{1,0:T(8,128)(2,1)S(1)} %get-tuple-element.11), channel_id=1, source_target_pairs={{8,16},{10,18},{16,24},{18,26},{24,28},{26,30},{28,20},{30,22},{20... | collective-permute-start | bytes 786440 | tf_op jit(solution)/shard_map/ppermute | solution.py:154
  74.9 13.5 %collective-permute-start.15 = (bf16[64,2048]{1,0:T(8,128)(2,1)S(1)}, bf16[64,2048]{1,0:T(8,128)(2,1)S(1)}, u32[]{:S(2)}, u32[]{:S(2)}) collective-permute-start(bf16[64,2048]{1,0:T(8,128)(2,1)S(1)} %get-tuple-element.12), channel_id=1, source_target_pairs={{8,0},{10,2},{16,8},{18,10},{24,16},{26,18},{28,24},{30,26},{20,28... | collective-permute-start | bytes 786440 | tf_op jit(solution)/shard_map/ppermute | solution.py:154
  88.4 2.3 %copy-start.10 = (bf16[128,2048]{1,0:T(8,128)(2,1)S(1)}, bf16[128,2048]{1,0:T(8,128)(2,1)}, u32[]{:S(2)}) copy-start(bf16[128,2048]{1,0:T(8,128)(2,1)} %copy-done.9) | copy-start | bytes 1572868
  88.6 16.0 %collective-permute-start.12 = (bf16[128,2048]{1,0:T(8,128)(2,1)S(1)}, bf16[128,2048]{1,0:T(8,128)(2,1)S(1)}, u32[]{:S(2)}, u32[]{:S(2)}) collective-permute-start(bf16[128,2048]{1,0:T(8,128)(2,1)S(1)} %get-tuple-element.9), channel_id=1, source_target_pairs={{8,16},{10,18},{16,24},{18,26},{24,28},{26,30},{28,20},{30,22},{20... | collective-permute-start | bytes 1572872 | tf_op jit(solution)/shard_map/ppermute | solution.py:154
  89.9 14.7 %collective-permute-start.16 = (bf16[128,2048]{1,0:T(8,128)(2,1)S(1)}, bf16[128,2048]{1,0:T(8,128)(2,1)S(1)}, u32[]{:S(2)}, u32[]{:S(2)}) collective-permute-start(bf16[128,2048]{1,0:T(8,128)(2,1)S(1)} %get-tuple-element.10), channel_id=1, source_target_pairs={{8,0},{10,2},{16,8},{18,10},{24,16},{26,18},{28,24},{30,26},{20,28... | collective-permute-start | bytes 1572872 | tf_op jit(solution)/shard_map/ppermute | solution.py:154
  104.6 2.4 %copy-start.6 = (bf16[128,2048]{1,0:T(8,128)(2,1)S(1)}, bf16[128,2048]{1,0:T(8,128)(2,1)}, u32[]{:S(2)}) copy-start(bf16[128,2048]{1,0:T(8,128)(2,1)} %copy-done.5) | copy-start | bytes 1572868
  104.6 2.4 %copy-start.8 = (bf16[128,2048]{1,0:T(8,128)(2,1)S(1)}, bf16[128,2048]{1,0:T(8,128)(2,1)}, u32[]{:S(2)}) copy-start(bf16[128,2048]{1,0:T(8,128)(2,1)} %copy-done.7) | copy-start | bytes 1572868
  104.9 14.9 %collective-permute-start.13 = (bf16[128,2048]{1,0:T(8,128)(2,1)S(1)}, bf16[128,2048]{1,0:T(8,128)(2,1)S(1)}, u32[]{:S(2)}, u32[]{:S(2)}) collective-permute-start(bf16[128,2048]{1,0:T(8,128)(2,1)S(1)} %get-tuple-element.7), channel_id=1, source_target_pairs={{8,16},{10,18},{16,24},{18,26},{24,28},{26,30},{28,20},{30,22},{20... | collective-permute-start | bytes 1572872 | tf_op jit(solution)/shard_map/ppermute | solution.py:154
  106.2 13.6 %collective-permute-start.17 = (bf16[128,2048]{1,0:T(8,128)(2,1)S(1)}, bf16[128,2048]{1,0:T(8,128)(2,1)S(1)}, u32[]{:S(2)}, u32[]{:S(2)}) collective-permute-start(bf16[128,2048]{1,0:T(8,128)(2,1)S(1)} %get-tuple-element.8), channel_id=1, source_target_pairs={{8,0},{10,2},{16,8},{18,10},{24,16},{26,18},{28,24},{30,26},{20,28... | collective-permute-start | bytes 1572872 | tf_op jit(solution)/shard_map/ppermute | solution.py:154
  119.8 2.4 %copy-start.1 = (bf16[1,2,2048,384]{3,2,1,0:T(8,128)(2,1)S(1)}, bf16[1,2,2048,384]{3,2,1,0:T(8,128)(2,1)}, u32[]{:S(2)}) copy-start(bf16[1,2,2048,384]{3,2,1,0:T(8,128)(2,1)} %param.9) | copy-start | bytes 9437188
  119.8 2.4 %copy-start.3 = (bf16[128,2048]{1,0:T(8,128)(2,1)S(1)}, bf16[128,2048]{1,0:T(8,128)(2,1)}, u32[]{:S(2)}) copy-start(bf16[128,2048]{1,0:T(8,128)(2,1)} %x_ref.1) | copy-start | bytes 1572868
  120.2 11.7 %collective-permute-start.14 = (bf16[128,2048]{1,0:T(8,128)(2,1)S(1)}, bf16[128,2048]{1,0:T(8,128)(2,1)S(1)}, u32[]{:S(2)}, u32[]{:S(2)}) collective-permute-start(bf16[128,2048]{1,0:T(8,128)(2,1)S(1)} %get-tuple-element.5), channel_id=1, source_target_pairs={{8,16},{10,18},{16,24},{18,26},{24,28},{26,30},{28,20},{30,22},{20... | collective-permute-start | bytes 1572872 | tf_op jit(solution)/shard_map/ppermute | solution.py:154
  121.5 10.4 %collective-permute-start.18 = (bf16[128,2048]{1,0:T(8,128)(2,1)S(1)}, bf16[128,2048]{1,0:T(8,128)(2,1)S(1)}, u32[]{:S(2)}, u32[]{:S(2)}) collective-permute-start(bf16[128,2048]{1,0:T(8,128)(2,1)S(1)} %get-tuple-element.6), channel_id=1, source_target_pairs={{8,0},{10,2},{16,8},{18,10},{24,16},{26,18},{28,24},{30,26},{20,28... | collective-permute-start | bytes 1572872 | tf_op jit(solution)/shard_map/ppermute | solution.py:154

commit v4 on v3

--- a/solution.py
+++ b/solution.py
@@ -56,84 +56,94 @@
     )(dense)
 
 
-def ffn_kernel(cycle, distances, x_ref, gate_ref, g0, u0, d0, g1, u1, d1, earlier_ref, out_ref):
-    i = pl.program_id(0)
-    x = x_ref[...]
+def halves_kernel(first_ref, second_ref, earlier_ref, top_ref, bottom_ref):
+    cut = top_ref.shape[0]
+    top_ref[...] = first_ref[:cut]
+    bottom_ref[...] = second_ref[cut:]
+
+
+def halves(first, second, earlier):
+    half = jax.ShapeDtypeStruct((first.shape[0] // 2, first.shape[1]), first.dtype)
+    vmem = pl.BlockSpec(memory_space=pltpu.VMEM)
+    return pl.pallas_call(
+        halves_kernel,
+        out_shape=(half, half),
+        in_specs=[vmem, vmem, pl.BlockSpec(memory_space=pl.ANY)],
+        out_specs=(vmem, vmem),
+    )(first, second, earlier)
+
+
+def ffn_kernel(cycle, distances, blocks_n, *refs):
+    x_refs, refs = refs[:blocks_n], refs[blocks_n:]
+    gate_ref, own, other = refs[0], refs[1:4], refs[4:7]
+    out_ref, x_ref, held, sems = refs[8], refs[9], refs[10:13], refs[13]
+    copies = []
+    for i in range(4):
+        slab = own if i < 2 else other
+        row = [
+            pltpu.make_async_copy(slab[k].at[i % 2], held[k].at[i], sems.at[i, k]) for k in range(3)
+        ]
+        for copy in row:
+            copy.start()
+        copies.append(row)
+
+    first = 0
+    for ref in x_refs:
+        x_ref[first : first + ref.shape[0]] = ref[...]
+        first += ref.shape[0]
+
     chips_n = len(cycle)
     chip = lax.axis_index("expert") // 2
     place = sum(jnp.where(chip == c, p, 0) for p, c in enumerate(cycle))
     lanes = lax.broadcasted_iota(jnp.int32, gate_ref.shape[1:], 1)
-    weights = []
+    weights = [[], []]
     for distance in distances:
         there = (place + distance + chips_n) % chips_n
         source = sum(jnp.where(there == p, c, 0) for p, c in enumerate(cycle))
         gates = gate_ref[(chip - source + chips_n) % chips_n].astype(jnp.float32)
-        picked = jnp.where(lanes == chip * 2 + i % 2, gates, 0.0)
-        weights.append(jnp.sum(picked, axis=1, keepdims=True))
-    weight = jnp.concatenate(weights)
-
-    def add(g_ref, u_ref, d_ref, first):
-        gate_h = jnp.dot(x, g_ref[0], preferred_element_type=jnp.float32)
-        up_h = jnp.dot(x, u_ref[0], preferred_element_type=jnp.float32)
-        hidden = gate_h / (1.0 + jnp.exp(-gate_h)) * up_h
-        hidden = hidden.astype(jnp.bfloat16)
-        part = jnp.dot(hidden, d_ref[0], preferred_element_type=jnp.float32) * weight
-
-        if first:
-
-            @pl.when(i == 0)
-            def _():
-                out_ref[...] = part
-
-            @pl.when(i > 0)
-            def _():
-                out_ref[...] += part
-
+        for j in range(2):
+            picked = jnp.where(lanes == chip * 2 + j, gates, 0.0)
+            weights[j].append(jnp.sum(picked, axis=1, keepdims=True))
+    weights = [jnp.concatenate(w) for w in weights]
+
+    x = x_ref[...]
+    for i in range(4):
+        copies[i][0].wait()
+        gate_h = jnp.dot(x, held[0][i], preferred_element_type=jnp.float32)
+        copies[i][1].wait()
+        up_h = jnp.dot(x, held[1][i], preferred_element_type=jnp.float32)
+        hidden = gate_h / (1.0 + jnp.exp(-gate_h)) * up_h * weights[i % 2]
+        copies[i][2].wait()
+        part = jnp.dot(hidden.astype(jnp.bfloat16), held[2][i], preferred_element_type=jnp.float32)
+        if i == 0:
+            out_ref[...] = part
         else:
             out_ref[...] += part
 
-    @pl.when(i < 2)
-    def _():
-        add(g0, u0, d0, True)
-
-    @pl.when(i >= 2)
-    def _():
-        add(g1, u1, d1, False)
-
-
-def ffn(cycle, distances, x, gates, own, other, earlier):
-    rows, width = x.shape
+
+def ffn(cycle, distances, blocks, gates, own, other, earlier):
+    rows, width = sum(b.shape[0] for b in blocks), blocks[0].shape[1]
     half = own[0].shape[2]
-
-    def early(shape):
-        return pl.BlockSpec((1,) + shape, lambda i: (jnp.minimum(i, 1), 0, 0))
-
-    def late(shape):
-        return pl.BlockSpec((1,) + shape, lambda i: (jnp.maximum(i - 2, 0), 0, 0))
-
-    flops = 4 * 2 * 3 * rows * width * half
-    moved = 4 * 3 * width * half * 2 + rows * width * 6
+    vmem, anywhere = pl.BlockSpec(memory_space=pltpu.VMEM), pl.BlockSpec(memory_space=pl.ANY)
     return pl.pallas_call(
-        functools.partial(ffn_kernel, cycle, distances),
-        grid=(4,),
+        functools.partial(ffn_kernel, cycle, distances, len(blocks)),
         out_shape=jax.ShapeDtypeStruct((rows, width), jnp.float32),
-        in_specs=[
-            pl.BlockSpec((rows, width), lambda i: (0, 0)),
-            pl.BlockSpec(gates.shape, lambda i: (0, 0, 0)),
-            early((width, half)),
-            early((width, half)),
-            early((half, width)),
-            late((width, half)),
-            late((width, half)),
-            late((half, width)),
-            pl.BlockSpec(memory_space=pl.ANY),
+        in_specs=[vmem] * len(blocks) + [vmem] + [anywhere] * 7,
+        out_specs=vmem,
+        scratch_shapes=[
+            pltpu.VMEM((rows, width), jnp.bfloat16),
+            pltpu.VMEM((4, width, half), jnp.bfloat16),
+            pltpu.VMEM((4, width, half), jnp.bfloat16),
+            pltpu.VMEM((4, half, width), jnp.bfloat16),
+            pltpu.SemaphoreType.DMA((4, 3)),
         ],
-        out_specs=pl.BlockSpec((rows, width), lambda i: (0, 0)),
         cost_estimate=pl.CostEstimate(
-            flops=flops, bytes_accessed=moved, transcendentals=4 * rows * half
+            flops=4 * 2 * 3 * rows * width * half,
+            bytes_accessed=4 * 3 * width * half * 2 + rows * width * 6,
+            transcendentals=4 * rows * half,
         ),
         compiler_params=pltpu.CompilerParams(vmem_limit_bytes=48 * 2**20),
-    )(x, gates, *own, *other, earlier)
+    )(*blocks, gates, *own, *other, earlier)
 
 
 def on_device(cycle, tokens, expert_ids, route_weight, w_gate, w_up, w_down):
@@ -164,16 +174,14 @@
     for s in range(1, far):
         from_left[s] = send(from_left[s - 1], right)
         from_right[s] = send(from_right[s - 1], left)
-    far_block = jnp.concatenate(
-        [send(from_left[far - 1][:cut], right), send(from_right[far - 1][cut:], left)]
-    )
     all_gates = share_gates(dense.astype(jnp.bfloat16), chips_n)
+    top, bottom = halves(from_left[far - 1], from_right[far - 1], all_gates)
+    top, bottom = send(top, right), send(bottom, left)
 
     def outputs(blocks, distances, earlier):
-        x = jnp.concatenate(blocks) if len(blocks) > 1 else blocks[0]
-        return ffn(cycle, distances, x, all_gates, own, other, earlier)
-
-    last = outputs([far_block], [far], far_block)
+        return ffn(cycle, distances, blocks, all_gates, own, other, earlier)
+
+    last = outputs([top, bottom], [far], top)
     for_left, for_right = {}, {}
     for s in range(1, far):
         both = outputs([from_left[s], from_right[s]], [-s, s], last)

time: 133 us -> 120 us (0.902)
  Pallas kernels: 69.2 us -> 59.1 us
  other arithmetic: 7.81 us -> 4.16 us
    pallas_call x5 -> x6, Pallas kernels: 57.3 us -> 45 us  [the longest x5 42.9 us: ffn(): pl.pallas_call(functools.partial(ffn_kernel, cycle, distances, len(blocks...]
    concatenate x4 -> x0, other arithmetic: 3.65 us -> none  [the longest x3 2.58 us: outputs(): x = jnp.concatenate(blocks) if len(blocks) > 1 else blocks[0]]
    unnamed x23 -> x17, local copies, waits for them, and re-layouts: 1.63 us -> 5.22 us
    slice x2 -> x0, local copies, waits for them, and re-layouts: 2.38 us -> none  [the longest x1 1.66 us: on_device(): from_left[far - 1][:cut]]
    pallas_call x1, Pallas kernels: 11.8 us -> 14.1 us  [share_gates(): pl.pallas_call(functools.partial(gates_kernel, chips_n), out_shape=jax.Sh...]
  transfers between devices with their start and end apart: 19 -> 19, of which waited for: 3 -> 6; matrix products, arithmetic and copies ran while one was open for 7% -> 3% of each run, Pallas kernels for 45% -> 44%
where the time goes in v4:
time: 120 us
  Pallas kernels  59.1 us (49%)
  waiting for transfers between devices  32.3 us (27%)
  starting transfers between devices  18.7 us (16%)
  local copies, waits for them, and re-layouts  5.37 us (4%)
  other arithmetic  4.16 us (3%)
    pallas_call x5, Pallas kernels, ffn(): pl.pallas_call(functools.partial(ffn_kernel, cycle, distances, len(blocks...  42.9 us
    ppermute x19, waiting for transfers between devices, on_device(): send = lambda value, pairs: lax.ppermute(value, 'expert', pairs)  32.3 us
    ppermute x19, starting transfers between devices, on_device(): send = lambda value, pairs: lax.ppermute(value, 'expert', pairs)  18.7 us
    pallas_call x1, Pallas kernels, share_gates(): pl.pallas_call(functools.partial(gates_kernel, chips_n), out_shape=jax.Sh...  14.1 us
    unnamed x17, local copies, waits for them, and re-layouts  5.22 us
  transfers between devices with their start and end apart: 19, of which 6 were waited for; matrix products, arithmetic and copies ran while one was open for 3% of the time, Pallas kernels for 44%

profile of v4, /device:TPU:0, one launch (start us, length us, event | category | flops | bytes accessed | tf_op | source)
XLA Modules:
  0.0 119.9 jit_solution(14923568112830372197)
XLA Ops:
  0.0 0.5 collective-permute-start
  0.5 0.5 collective-permute-start.2
  1.0 2.6 %collective-permute-start.3 = (bf16[128,2048]{1,0:T(8,128)(2,1)}, bf16[128,2048]{1,0:T(8,128)(2,1)S(1)}, u32[]{:S(2)}, u32[]{:S(2)}) collective-permute-start(bf16[128,2048]{1,0:T(8,128)(2,1)} %refs_0_.1), channel_id=1, source_target_pairs={{8,16},{10,18},{16,24},{18,26},{24,28},{26,30},{28,20},{30,22},{20... | collective-permute-start | bytes 1572872 | tf_op jit(solution)/shard_map/ppermute | solution.py:164
  3.5 12.7 %collective-permute-done.3.refs_0_ = bf16[128,2048]{1,0:T(8,128)(2,1)S(1)} collective-permute-done((bf16[128,2048]{1,0:T(8,128)(2,1)}, bf16[128,2048]{1,0:T(8,128)(2,1)S(1)}, u32[]{:S(2)}, u32[]{:S(2)}) %collective-permute-start.3) | collective-permute-done | bytes 524320 | tf_op jit(solution)/shard_map/ppermute | solution.py:164
  16.3 1.8 %collective-permute-start.4 = (bf16[128,2048]{1,0:T(8,128)(2,1)S(1)}, bf16[128,2048]{1,0:T(8,128)(2,1)S(1)}, u32[]{:S(2)}, u32[]{:S(2)}) collective-permute-start(bf16[128,2048]{1,0:T(8,128)(2,1)S(1)} %collective-permute-done.3.refs_0_), channel_id=1, source_target_pairs={{8,16},{10,18},{16,24},{18,26},{24,28},{26,30},{28,20},{30,22},{20... | collective-permute-start | bytes 1572872 | tf_op jit(solution)/shard_map/ppermute | solution.py:164
  18.3 11.7 %collective-permute-done.4.refs_0_ = bf16[128,2048]{1,0:T(8,128)(2,1)S(1)} collective-permute-done((bf16[128,2048]{1,0:T(8,128)(2,1)S(1)}, bf16[128,2048]{1,0:T(8,128)(2,1)S(1)}, u32[]{:S(2)}, u32[]{:S(2)}) %collective-permute-start.4) | collective-permute-done | bytes 524320 | tf_op jit(solution)/shard_map/ppermute | solution.py:164
  30.0 1.6 %collective-permute-start.5 = (bf16[128,2048]{1,0:T(8,128)(2,1)S(1)}, bf16[128,2048]{1,0:T(8,128)(2,1)S(1)}, u32[]{:S(2)}, u32[]{:S(2)}) collective-permute-start(bf16[128,2048]{1,0:T(8,128)(2,1)S(1)} %collective-permute-done.4.refs_0_), channel_id=1, source_target_pairs={{8,16},{10,18},{16,24},{18,26},{24,28},{26,30},{28,20},{30,22},{20... | collective-permute-start | bytes 1572872 | tf_op jit(solution)/shard_map/ppermute | solution.py:164
  31.6 0.4 collective-permute-start.8
  32.1 0.7 reduce_sum.18
  32.8 0.7 fusion.6
  33.6 0.8 copy.9
  34.4 1.0 select_reduce_fusion.gate_ref
  35.3 14.1 %shard_map.64.earlier_ref.refs_2_.refs_1_ = bf16[8,128,128]{2,1,0:T(8,128)(2,1)} custom-call(bf16[128,128]{1,0:T(8,128)(2,1)} %select_reduce_fusion.gate_ref), custom_call_target="tpu_custom_call" | custom-call | tf_op jit(solution)/shard_map/pallas_call | solution.py:49
  49.5 0.8 copy-done.3
  50.3 0.8 copy-done.5
  51.1 2.0 %shard_map.65 = (bf16[64,2048]{1,0:T(8,128)(2,1)}, bf16[64,2048]{1,0:T(8,128)(2,1)}) custom-call(bf16[128,2048]{1,0:T(8,128)(2,1)} %copy-done.3, bf16[128,2048]{1,0:T(8,128)(2,1)} %copy-done.5, bf16[8,128,128]{2,1,0:T(8,128)(2,1)} %shard_map.64.earlier_ref.refs_2_.refs_1_), custom_call_target="tpu_custom_call" | custom-call | tf_op jit(solution)/shard_map/pallas_call | solution.py:68
  53.1 2.8 %collective-permute-start.10 = (bf16[64,2048]{1,0:T(8,128)(2,1)}, bf16[64,2048]{1,0:T(8,128)(2,1)S(1)}, u32[]{:S(2)}, u32[]{:S(2)}) collective-permute-start(bf16[64,2048]{1,0:T(8,128)(2,1)} %get-tuple-element.8), channel_id=1, source_target_pairs={{8,0},{10,2},{16,8},{18,10},{24,16},{26,18},{28,24},{30,26},{20,28... | collective-permute-start | bytes 786440 | tf_op jit(solution)/shard_map/ppermute | solution.py:164
  55.9 4.2 %collective-permute-done.10.refs_1_ = bf16[64,2048]{1,0:T(8,128)(2,1)S(1)} collective-permute-done((bf16[64,2048]{1,0:T(8,128)(2,1)}, bf16[64,2048]{1,0:T(8,128)(2,1)S(1)}, u32[]{:S(2)}, u32[]{:S(2)}) %collective-permute-start.10) | collective-permute-done | bytes 262176 | tf_op jit(solution)/shard_map/ppermute | solution.py:164
  60.1 2.4 %collective-permute-done.9.refs_0_.refs_9_ = bf16[64,2048]{1,0:T(8,128)(2,1)S(1)} collective-permute-done((bf16[64,2048]{1,0:T(8,128)(2,1)}, bf16[64,2048]{1,0:T(8,128)(2,1)S(1)}, u32[]{:S(2)}, u32[]{:S(2)}) %collective-permute-start.9) | collective-permute-done | bytes 262176 | tf_op jit(solution)/shard_map/ppermute | solution.py:164
  62.5 1.9 %copy-done = bf16[1,2,2048,384]{3,2,1,0:T(8,128)(2,1)S(1)} copy-done((bf16[1,2,2048,384]{3,2,1,0:T(8,128)(2,1)S(1)}, bf16[1,2,2048,384]{3,2,1,0:T(8,128)(2,1)}, u32[]{:S(2)}) %copy-start) | copy-done | bytes 3145752
  64.4 0.9 copy-done.2
  65.4 6.5 %shard_map.66.refs_9_ = f32[128,2048]{1,0:T(8,128)S(1)} custom-call(bf16[64,2048]{1,0:T(8,128)(2,1)S(1)} %collective-permute-done.9.refs_0_.refs_9_, bf16[64,2048]{1,0:T(8,128)(2,1)S(1)} %collective-permute-done.10.refs_1_, bf16[8,128,128]{2,1,0:T(8,128)(2,1)S(1)} %copy-done.2, bf16[2,2048,384]{2,1,0:T(8,128)(2,1)S(1)} %bitcast.7, ...), custom_call_target="tpu_custom_call" | custom-call | flops 2415919104 | bytes 20447232 | tf_op jit(solution)/shard_map/pallas_call | solution.py:128
  72.0 2.0 %collective-permute-start.15 = (bf16[64,2048]{1,0:T(8,128)(2,1)S(1)}, bf16[64,2048]{1,0:T(8,128)(2,1)S(1)}, u32[]{:S(2)}, u32[]{:S(2)}) collective-permute-start(bf16[64,2048]{1,0:T(8,128)(2,1)S(1)} %get-tuple-element.16), channel_id=1, source_target_pairs={{8,0},{10,2},{16,8},{18,10},{24,16},{26,18},{28,24},{30,26},{20,28... | collective-permute-start | bytes 786440 | tf_op jit(solution)/shard_map/ppermute | solution.py:164
  74.0 10.1 %shard_map.67 = f32[256,2048]{1,0:T(8,128)S(1)} custom-call(bf16[128,2048]{1,0:T(8,128)(2,1)S(1)} %copy-done.4, bf16[128,2048]{1,0:T(8,128)(2,1)S(1)} %copy-done.6, bf16[8,128,128]{2,1,0:T(8,128)(2,1)S(1)} %copy-done.2, bf16[2,2048,384]{2,1,0:T(8,128)(2,1)} %bitcast.4, bf16[2,2048,384]{2,1,0:T(8,128)(2,1)} %bitcast.11, bf16[2,384,2048]{2,1,0:T(8,128)(2,1)} %bitcast.17, ...), custom_call_target="tpu_custom_call" | custom-call | flops 4831838208 | bytes 22020096 | tf_op jit(solution)/shard_map/pallas_call | solution.py:128
  84.6 1.8 %collective-permute-start.16 = (bf16[128,2048]{1,0:T(8,128)(2,1)S(1)}, bf16[128,2048]{1,0:T(8,128)(2,1)S(1)}, u32[]{:S(2)}, u32[]{:S(2)}) collective-permute-start(bf16[128,2048]{1,0:T(8,128)(2,1)S(1)} %get-tuple-element.14), channel_id=1, source_target_pairs={{8,0},{10,2},{16,8},{18,10},{24,16},{26,18},{28,24},{30,26},{20,28... | collective-permute-start | bytes 1572872 | tf_op jit(solution)/shard_map/ppermute | solution.py:164
  86.4 10.1 %shard_map.68 = f32[256,2048]{1,0:T(8,128)S(1)} custom-call(bf16[128,2048]{1,0:T(8,128)(2,1)S(1)} %collective-permute-done.4.refs_0_, bf16[128,2048]{1,0:T(8,128)(2,1)S(1)} %collective-permute-done.7.refs_1_, bf16[8,128,128]{2,1,0:T(8,128)(2,1)S(1)} %copy-done.2, bf16[2,2048,384]{2,1,0:T(8,128)(2,1)} %bitcast.5, bf16[2,2048,384]{2,1,0:T(8,128)(2,1)} %bitcast.12, ...), custom_call_target="tpu_custom_call" | custom-call | flops 4831838208 | bytes 22020096 | tf_op jit(solution)/shard_map/pallas_call | solution.py:128
  97.1 1.7 %collective-permute-start.17 = (bf16[128,2048]{1,0:T(8,128)(2,1)S(1)}, bf16[128,2048]{1,0:T(8,128)(2,1)S(1)}, u32[]{:S(2)}, u32[]{:S(2)}) collective-permute-start(bf16[128,2048]{1,0:T(8,128)(2,1)S(1)} %get-tuple-element.12), channel_id=1, source_target_pairs={{8,0},{10,2},{16,8},{18,10},{24,16},{26,18},{28,24},{30,26},{20,28... | collective-permute-start | bytes 1572872 | tf_op jit(solution)/shard_map/ppermute | solution.py:164
  98.9 10.1 %shard_map.70 = f32[256,2048]{1,0:T(8,128)S(1)} custom-call(bf16[128,2048]{1,0:T(8,128)(2,1)S(1)} %collective-permute-done.3.refs_0_, bf16[128,2048]{1,0:T(8,128)(2,1)S(1)} %collective-permute-done.6.refs_1_, bf16[8,128,128]{2,1,0:T(8,128)(2,1)S(1)} %copy-done.2, bf16[2,2048,384]{2,1,0:T(8,128)(2,1)} %bitcast.6, bf16[2,2048,384]{2,1,0:T(8,128)(2,1)} %bitcast.13, ...), custom_call_target="tpu_custom_call" | custom-call | flops 4831838208 | bytes 22020096 | tf_op jit(solution)/shard_map/pallas_call | solution.py:128
  109.7 1.7 %collective-permute-start.18 = (bf16[128,2048]{1,0:T(8,128)(2,1)S(1)}, bf16[128,2048]{1,0:T(8,128)(2,1)S(1)}, u32[]{:S(2)}, u32[]{:S(2)}) collective-permute-start(bf16[128,2048]{1,0:T(8,128)(2,1)S(1)} %get-tuple-element.10), channel_id=1, source_target_pairs={{8,0},{10,2},{16,8},{18,10},{24,16},{26,18},{28,24},{30,26},{20,28... | collective-permute-start | bytes 1572872 | tf_op jit(solution)/shard_map/ppermute | solution.py:164
  111.4 6.3 %shard_map.69 = f32[128,2048]{1,0:T(8,128)S(1)} custom-call(bf16[128,2048]{1,0:T(8,128)(2,1)S(1)} %copy-done.7, bf16[8,128,128]{2,1,0:T(8,128)(2,1)S(1)} %copy-done.2, bf16[2,2048,384]{2,1,0:T(8,128)(2,1)S(1)} %bitcast.8, bf16[2,2048,384]{2,1,0:T(8,128)(2,1)} %bitcast.14, bf16[2,384,2048]{2,1,0:T(8,128)(2,1)} %bitcast.20, ...), custom_call_target="tpu_custom_call" | custom-call | flops 2415919104 | bytes 20447232 | tf_op jit(solution)/shard_map/pallas_call | solution.py:128
  117.6 0.9 collective-permute-done.14
  118.9 1.0 add_convert_fusion
  (40 shorter events, 2.7 us)
Async XLA Ops:
  0.0 62.5 %collective-permute-start = (bf16[2,2048,384]{2,1,0:T(8,128)(2,1)}, bf16[2,2048,384]{2,1,0:T(8,128)(2,1)}, u32[]{:S(2)}, u32[]{:S(2)}) collective-permute-start(bf16[2,2048,384]{2,1,0:T(8,128)(2,1)} %bitcast.3), channel_id=1, source_target_pairs={{0,2},{2,0},{4,6},{6,4},{8,10},{10,8},{12,14},{14,12},{16,18},{18,... | collective-permute-start | bytes 9437192 | tf_op jit(solution)/shard_map/ppermute | solution.py:164
  0.5 62.1 %collective-permute-start.1 = (bf16[2,2048,384]{2,1,0:T(8,128)(2,1)}, bf16[2,2048,384]{2,1,0:T(8,128)(2,1)}, u32[]{:S(2)}, u32[]{:S(2)}) collective-permute-start(bf16[2,2048,384]{2,1,0:T(8,128)(2,1)} %bitcast.9), channel_id=1, source_target_pairs={{0,2},{2,0},{4,6},{6,4},{8,10},{10,8},{12,14},{14,12},{16,18},{18,... | collective-permute-start | bytes 9437192 | tf_op jit(solution)/shard_map/ppermute | solution.py:164
  0.5 62.0 %collective-permute-start.2 = (bf16[2,384,2048]{2,1,0:T(8,128)(2,1)}, bf16[2,384,2048]{2,1,0:T(8,128)(2,1)}, u32[]{:S(2)}, u32[]{:S(2)}) collective-permute-start(bf16[2,384,2048]{2,1,0:T(8,128)(2,1)} %bitcast.15), channel_id=1, source_target_pairs={{0,2},{2,0},{4,6},{6,4},{8,10},{10,8},{12,14},{14,12},{16,18},{18,... | collective-permute-start | bytes 9437192 | tf_op jit(solution)/shard_map/ppermute | solution.py:164
  1.0 15.3 %collective-permute-start.3 = (bf16[128,2048]{1,0:T(8,128)(2,1)}, bf16[128,2048]{1,0:T(8,128)(2,1)S(1)}, u32[]{:S(2)}, u32[]{:S(2)}) collective-permute-start(bf16[128,2048]{1,0:T(8,128)(2,1)} %refs_0_.1), channel_id=1, source_target_pairs={{8,16},{10,18},{16,24},{18,26},{24,28},{26,30},{28,20},{30,22},{20... | collective-permute-start | bytes 1572872 | tf_op jit(solution)/shard_map/ppermute | solution.py:164
  3.5 14.6 %collective-permute-start.6 = (bf16[128,2048]{1,0:T(8,128)(2,1)}, bf16[128,2048]{1,0:T(8,128)(2,1)S(1)}, u32[]{:S(2)}, u32[]{:S(2)}) collective-permute-start(bf16[128,2048]{1,0:T(8,128)(2,1)} %refs_0_.1), channel_id=1, source_target_pairs={{8,0},{10,2},{16,8},{18,10},{24,16},{26,18},{28,24},{30,26},{20,28... | collective-permute-start | bytes 1572872 | tf_op jit(solution)/shard_map/ppermute | solution.py:164
  16.3 13.8 %collective-permute-start.4 = (bf16[128,2048]{1,0:T(8,128)(2,1)S(1)}, bf16[128,2048]{1,0:T(8,128)(2,1)S(1)}, u32[]{:S(2)}, u32[]{:S(2)}) collective-permute-start(bf16[128,2048]{1,0:T(8,128)(2,1)S(1)} %collective-permute-done.3.refs_0_), channel_id=1, source_target_pairs={{8,16},{10,18},{16,24},{18,26},{24,28},{26,30},{28,20},{30,22},{20... | collective-permute-start | bytes 1572872 | tf_op jit(solution)/shard_map/ppermute | solution.py:164
  18.1 13.6 %collective-permute-start.7 = (bf16[128,2048]{1,0:T(8,128)(2,1)S(1)}, bf16[128,2048]{1,0:T(8,128)(2,1)S(1)}, u32[]{:S(2)}, u32[]{:S(2)}) collective-permute-start(bf16[128,2048]{1,0:T(8,128)(2,1)S(1)} %collective-permute-done.6.refs_1_), channel_id=1, source_target_pairs={{8,0},{10,2},{16,8},{18,10},{24,16},{26,18},{28,24},{30,26},{20,28... | collective-permute-start | bytes 1572872 | tf_op jit(solution)/shard_map/ppermute | solution.py:164
  30.0 19.4 %collective-permute-start.5 = (bf16[128,2048]{1,0:T(8,128)(2,1)S(1)}, bf16[128,2048]{1,0:T(8,128)(2,1)S(1)}, u32[]{:S(2)}, u32[]{:S(2)}) collective-permute-start(bf16[128,2048]{1,0:T(8,128)(2,1)S(1)} %collective-permute-done.4.refs_0_), channel_id=1, source_target_pairs={{8,16},{10,18},{16,24},{18,26},{24,28},{26,30},{28,20},{30,22},{20... | collective-permute-start | bytes 1572872 | tf_op jit(solution)/shard_map/ppermute | solution.py:164
  31.6 17.9 %collective-permute-start.8 = (bf16[128,2048]{1,0:T(8,128)(2,1)S(1)}, bf16[128,2048]{1,0:T(8,128)(2,1)S(1)}, u32[]{:S(2)}, u32[]{:S(2)}) collective-permute-start(bf16[128,2048]{1,0:T(8,128)(2,1)S(1)} %collective-permute-done.7.refs_1_), channel_id=1, source_target_pairs={{8,0},{10,2},{16,8},{18,10},{24,16},{26,18},{28,24},{30,26},{20,28... | collective-permute-start | bytes 1572872 | tf_op jit(solution)/shard_map/ppermute | solution.py:164
  49.5 0.8 copy-start.3
  50.3 0.8 copy-start.5
  53.1 7.0 %collective-permute-start.10 = (bf16[64,2048]{1,0:T(8,128)(2,1)}, bf16[64,2048]{1,0:T(8,128)(2,1)S(1)}, u32[]{:S(2)}, u32[]{:S(2)}) collective-permute-start(bf16[64,2048]{1,0:T(8,128)(2,1)} %get-tuple-element.8), channel_id=1, source_target_pairs={{8,0},{10,2},{16,8},{18,10},{24,16},{26,18},{28,24},{30,26},{20,28... | collective-permute-start | bytes 786440 | tf_op jit(solution)/shard_map/ppermute | solution.py:164
  55.9 6.6 %collective-permute-start.9 = (bf16[64,2048]{1,0:T(8,128)(2,1)}, bf16[64,2048]{1,0:T(8,128)(2,1)S(1)}, u32[]{:S(2)}, u32[]{:S(2)}) collective-permute-start(bf16[64,2048]{1,0:T(8,128)(2,1)} %get-tuple-element.7), channel_id=1, source_target_pairs={{8,16},{10,18},{16,24},{18,26},{24,28},{26,30},{28,20},{30,22},{20... | collective-permute-start | bytes 786440 | tf_op jit(solution)/shard_map/ppermute | solution.py:164
  62.5 1.9 %copy-start = (bf16[1,2,2048,384]{3,2,1,0:T(8,128)(2,1)S(1)}, bf16[1,2,2048,384]{3,2,1,0:T(8,128)(2,1)}, u32[]{:S(2)}) copy-start(bf16[1,2,2048,384]{3,2,1,0:T(8,128)(2,1)} %param.9) | copy-start | bytes 9437188
  64.4 0.9 copy-start.2
  65.4 8.7 %copy-start.4 = (bf16[128,2048]{1,0:T(8,128)(2,1)S(1)}, bf16[128,2048]{1,0:T(8,128)(2,1)}, u32[]{:S(2)}) copy-start(bf16[128,2048]{1,0:T(8,128)(2,1)} %copy-done.3) | copy-start | bytes 1572868
  65.4 8.7 %copy-start.6 = (bf16[128,2048]{1,0:T(8,128)(2,1)S(1)}, bf16[128,2048]{1,0:T(8,128)(2,1)}, u32[]{:S(2)}) copy-start(bf16[128,2048]{1,0:T(8,128)(2,1)} %copy-done.5) | copy-start | bytes 1572868
  71.9 12.2 %collective-permute-start.11 = (bf16[64,2048]{1,0:T(8,128)(2,1)S(1)}, bf16[64,2048]{1,0:T(8,128)(2,1)S(1)}, u32[]{:S(2)}, u32[]{:S(2)}) collective-permute-start(bf16[64,2048]{1,0:T(8,128)(2,1)S(1)} %get-tuple-element.15), channel_id=1, source_target_pairs={{8,16},{10,18},{16,24},{18,26},{24,28},{26,30},{28,20},{30,22},{20... | collective-permute-start | bytes 786440 | tf_op jit(solution)/shard_map/ppermute | solution.py:164
  72.0 12.1 %collective-permute-start.15 = (bf16[64,2048]{1,0:T(8,128)(2,1)S(1)}, bf16[64,2048]{1,0:T(8,128)(2,1)S(1)}, u32[]{:S(2)}, u32[]{:S(2)}) collective-permute-start(bf16[64,2048]{1,0:T(8,128)(2,1)S(1)} %get-tuple-element.16), channel_id=1, source_target_pairs={{8,0},{10,2},{16,8},{18,10},{24,16},{26,18},{28,24},{30,26},{20,28... | collective-permute-start | bytes 786440 | tf_op jit(solution)/shard_map/ppermute | solution.py:164
  84.3 12.2 %collective-permute-start.12 = (bf16[128,2048]{1,0:T(8,128)(2,1)S(1)}, bf16[128,2048]{1,0:T(8,128)(2,1)S(1)}, u32[]{:S(2)}, u32[]{:S(2)}) collective-permute-start(bf16[128,2048]{1,0:T(8,128)(2,1)S(1)} %get-tuple-element.13), channel_id=1, source_target_pairs={{8,16},{10,18},{16,24},{18,26},{24,28},{26,30},{28,20},{30,22},{20... | collective-permute-start | bytes 1572872 | tf_op jit(solution)/shard_map/ppermute | solution.py:164
  84.6 11.9 %collective-permute-start.16 = (bf16[128,2048]{1,0:T(8,128)(2,1)S(1)}, bf16[128,2048]{1,0:T(8,128)(2,1)S(1)}, u32[]{:S(2)}, u32[]{:S(2)}) collective-permute-start(bf16[128,2048]{1,0:T(8,128)(2,1)S(1)} %get-tuple-element.14), channel_id=1, source_target_pairs={{8,0},{10,2},{16,8},{18,10},{24,16},{26,18},{28,24},{30,26},{20,28... | collective-permute-start | bytes 1572872 | tf_op jit(solution)/shard_map/ppermute | solution.py:164
  96.8 12.2 %collective-permute-start.13 = (bf16[128,2048]{1,0:T(8,128)(2,1)S(1)}, bf16[128,2048]{1,0:T(8,128)(2,1)S(1)}, u32[]{:S(2)}, u32[]{:S(2)}) collective-permute-start(bf16[128,2048]{1,0:T(8,128)(2,1)S(1)} %get-tuple-element.11), channel_id=1, source_target_pairs={{8,16},{10,18},{16,24},{18,26},{24,28},{26,30},{28,20},{30,22},{20... | collective-permute-start | bytes 1572872 | tf_op jit(solution)/shard_map/ppermute | solution.py:164
  97.1 11.9 %collective-permute-start.17 = (bf16[128,2048]{1,0:T(8,128)(2,1)S(1)}, bf16[128,2048]{1,0:T(8,128)(2,1)S(1)}, u32[]{:S(2)}, u32[]{:S(2)}) collective-permute-start(bf16[128,2048]{1,0:T(8,128)(2,1)S(1)} %get-tuple-element.12), channel_id=1, source_target_pairs={{8,0},{10,2},{16,8},{18,10},{24,16},{26,18},{28,24},{30,26},{20,28... | collective-permute-start | bytes 1572872 | tf_op jit(solution)/shard_map/ppermute | solution.py:164
  109.0 2.4 %copy-start.1 = (bf16[1,2,2048,384]{3,2,1,0:T(8,128)(2,1)S(1)}, bf16[1,2,2048,384]{3,2,1,0:T(8,128)(2,1)}, u32[]{:S(2)}) copy-start(bf16[1,2,2048,384]{3,2,1,0:T(8,128)(2,1)} %param.9) | copy-start | bytes 9437188
  109.0 2.4 %copy-start.7 = (bf16[128,2048]{1,0:T(8,128)(2,1)S(1)}, bf16[128,2048]{1,0:T(8,128)(2,1)}, u32[]{:S(2)}) copy-start(bf16[128,2048]{1,0:T(8,128)(2,1)} %refs_0_.1) | copy-start | bytes 1572868
  109.3 9.2 %collective-permute-start.14 = (bf16[128,2048]{1,0:T(8,128)(2,1)S(1)}, bf16[128,2048]{1,0:T(8,128)(2,1)S(1)}, u32[]{:S(2)}, u32[]{:S(2)}) collective-permute-start(bf16[128,2048]{1,0:T(8,128)(2,1)S(1)} %get-tuple-element.9), channel_id=1, source_target_pairs={{8,16},{10,18},{16,24},{18,26},{24,28},{26,30},{28,20},{30,22},{20... | collective-permute-start | bytes 1572872 | tf_op jit(solution)/shard_map/ppermute | solution.py:164
  109.7 9.2 %collective-permute-start.18 = (bf16[128,2048]{1,0:T(8,128)(2,1)S(1)}, bf16[128,2048]{1,0:T(8,128)(2,1)S(1)}, u32[]{:S(2)}, u32[]{:S(2)}) collective-permute-start(bf16[128,2048]{1,0:T(8,128)(2,1)S(1)} %get-tuple-element.10), channel_id=1, source_target_pairs={{8,0},{10,2},{16,8},{18,10},{24,16},{26,18},{28,24},{30,26},{20,28... | collective-permute-start | bytes 1572872 | tf_op jit(solution)/shard_map/ppermute | solution.py:164
